TPU v7x, 32 devices: a whole 2x2x4 slice. The times are simulated.
32 devices in a mesh: seq: 4 (over y, x), dp: 8 (over z, core).
Axes of the slice: x: 2, y: 2, z: 4, core: 2. Of those that a mesh axis runs over, the one named last changes fastest.
Arguments:
- tokens: float32 [64, 512, 768], P('dp', 'seq')
- positions: int32 [64, 128], P('dp'), may hold values from 0 to 511, as said below
- counts: int32 [64], P('dp'), may hold values from 44 to 128, as said below
- cotangent: float32 [64, 128, 768], P('dp'), may hold values from -6 to 6
- attn_weights: float32 [4, 768, 768], P(None, ('seq', 'dp'))
- ffn_in: float32 [768, 3072], P(('seq', 'dp')), may hold values from -0.21875 to 0.21875
- ffn_out: float32 [3072, 768], P(('seq', 'dp')), may hold values from -0.109375 to 0.109375
- vectors: float32 [9216], P(('seq', 'dp'))
- attn_first: float32 [4, 768, 768], P(None, ('seq', 'dp')), may hold values from -0.005859375 to 0.005859375
- ffn_in_first: float32 [768, 3072], P(('seq', 'dp')), may hold values from -0.005859375 to 0.005859375
- ffn_out_first: float32 [3072, 768], P(('seq', 'dp')), may hold values from -0.005859375 to 0.005859375
- vector_first: float32 [9216], P(('seq', 'dp')), may hold values from -0.0234375 to 0.0234375
- attn_second: float32 [4, 768, 768], P(None, ('seq', 'dp')), may hold values from 7.0550676e-08 to 1.1288108e-06
- ffn_in_second: float32 [768, 3072], P(('seq', 'dp')), may hold values from 7.0550676e-08 to 1.1288108e-06
- ffn_out_second: float32 [3072, 768], P(('seq', 'dp')), may hold values from 7.0550676e-08 to 1.1288108e-06
- vector_second: float32 [9216], P(('seq', 'dp')), may hold values from 1.1288108e-06 to 1.8060973e-05
Outputs:
- output: float32 [64, 512, 768], P('dp', 'seq')
- grad_tokens: float32 [64, 512, 768], P('dp', 'seq')
- grad_attn: float32 [4, 768, 768], P(None, ('seq', 'dp'))
- grad_ffn_in: float32 [768, 3072], P(('seq', 'dp'))
- grad_ffn_out: float32 [3072, 768], P(('seq', 'dp'))
- grad_vectors: float32 [9216], P(('seq', 'dp'))
- new_attn_first: float32 [4, 768, 768], P(None, ('seq', 'dp'))
- new_ffn_in_first: float32 [768, 3072], P(('seq', 'dp'))
- new_ffn_out_first: float32 [3072, 768], P(('seq', 'dp'))
- new_vector_first: float32 [9216], P(('seq', 'dp'))
- new_attn_second: float32 [4, 768, 768], P(None, ('seq', 'dp'))
- new_ffn_in_second: float32 [768, 3072], P(('seq', 'dp'))
- new_ffn_out_second: float32 [3072, 768], P(('seq', 'dp'))
- new_vector_second: float32 [9216], P(('seq', 'dp'))
- new_attn: float32 [4, 768, 768], P(None, ('seq', 'dp'))
- new_ffn_in: float32 [768, 3072], P(('seq', 'dp'))
- new_ffn_out: float32 [3072, 768], P(('seq', 'dp'))
- new_vectors: float32 [9216], P(('seq', 'dp'))
- low_attn: bfloat16 [4, 768, 768], P(None, ('seq', 'dp'))
- low_ffn_in: bfloat16 [768, 3072], P(('seq', 'dp'))
- low_ffn_out: bfloat16 [3072, 768], P(('seq', 'dp'))
- lamb_norms: float32 [2, 6], replicated
- trust_ratio: float32 [6], replicated
- grad_norm: float32 [], replicated
Inputs may be any that keep to these rules, and one draw needn't show every extreme that they name: Each row lists distinct positions of its sequence; only the first counts[s] entries of row s are masked positions, the others are ignored. `counts`: some sequence has exactly 128 masked positions.
All inputs are finite; a program needn't handle non-finite values.
Results may differ from a plain program's by a relative error of at most 0.014.
The roundings to bfloat16 on the way count: a program that leaves them out, or rounds other values in their place, can miss the bound.
Values may be sent and summed in bfloat16 or wider, within the bound.
A program may use at most 256 MiB of HBM per device.

v0:
```python
import jax
import jax.numpy as jnp
from jax import lax
from jax.sharding import PartitionSpec as P

H = 12
HD = 64
STEP = 5


decay_rate = 0.5
step_rate = 0.3
weight_decay = 0.01
adam_eps = 1e-06
norm_eps = 1e-12


def layer_norm(hidden, gain_vec, shift_vec):
    center = hidden - jnp.mean(hidden, -1, keepdims=True)
    spread = jnp.mean(center * center, -1, keepdims=True)
    return center * lax.rsqrt(spread + norm_eps) * gain_vec + shift_vec


def gelu_exact(inputs):
    return jax.nn.gelu(inputs, approximate=False)


def column_sum(inputs):
    return jnp.sum(inputs.astype(jnp.float32), axis=0)


def adam_direction(first_old, second_old, clipped):
    first_new = decay_rate * first_old + (1.0 - decay_rate) * clipped
    second_new = decay_rate * second_old + (1.0 - decay_rate) * clipped * clipped
    correct = 1.0 - decay_rate**STEP
    direction = first_new / correct / (jnp.sqrt(second_new / correct) + adam_eps)
    return (first_new, second_new, direction)


def body(
    tokens,
    positions,
    counts,
    cotangent,
    attn_weights,
    ffn_in,
    ffn_out,
    vectors,
    attn_first,
    ffn_in_first,
    ffn_out_first,
    vector_first,
    attn_second,
    ffn_in_second,
    ffn_out_second,
    vector_second,
):
    bf16 = jnp.bfloat16
    f32 = jnp.float32
    sequences, block_size, model_width = tokens.shape
    head_count = H
    head_size = HD
    length = block_size * lax.axis_size("seq")
    token_rows = sequences * block_size
    score_scale = head_size ** (-0.5)
    gathered = (
        lax.all_gather(attn_weights.astype(bf16), ("seq", "dp"), axis=1, tiled=True),
        lax.all_gather(ffn_in.astype(bf16), ("seq", "dp"), axis=0, tiled=True),
        lax.all_gather(ffn_out.astype(bf16), ("seq", "dp"), axis=0, tiled=True),
        lax.all_gather(vectors.astype(bf16), ("seq", "dp"), axis=0, tiled=True),
    )
    attn_full, in_full, out_full, vec_full = gathered
    vec_float = vec_full.astype(f32)
    pieces = [vec_float[index * model_width : (index + 1) * model_width] for index in range(8)]
    bias_query, bias_value, bias_out, bias_feed, gain_one, shift_one, gain_two, shift_two = pieces
    bias_inner = vec_float[8 * model_width :]
    flat_tokens = tokens.reshape(token_rows, model_width)
    flat_low = flat_tokens.astype(bf16)
    projected = jnp.einsum("rd,kde->kre", flat_low, attn_full[:3], preferred_element_type=f32)
    query_low = (projected[0] + bias_query).astype(bf16)
    key_low = projected[1].astype(bf16)
    value_low = (projected[2] + bias_value).astype(bf16)
    block_shape = (sequences, block_size, model_width)
    all_keys, all_values = (
        lax.all_gather(key_low.reshape(block_shape), "seq", axis=1, tiled=True),
        lax.all_gather(value_low.reshape(block_shape), "seq", axis=1, tiled=True),
    )
    query_heads = query_low.reshape(sequences, block_size, head_count, head_size)
    key_heads = all_keys.reshape(sequences, length, head_count, head_size)
    value_heads = all_values.reshape(sequences, length, head_count, head_size)
    scores = (
        jnp.einsum("sqhe,skhe->shqk", query_heads, key_heads, preferred_element_type=f32)
        * score_scale
    )
    row_top = jnp.max(scores, -1, keepdims=True)
    exponent = jnp.exp(scores - row_top)
    row_total = jnp.sum(exponent, -1, keepdims=True)
    attn_probs = exponent / row_total
    probs_low = attn_probs.astype(bf16)
    context = jnp.einsum("shqk,skhe->sqhe", probs_low, value_heads, preferred_element_type=f32)
    context_low = context.reshape(token_rows, model_width).astype(bf16)
    attended = jnp.dot(context_low, attn_full[3], preferred_element_type=f32) + bias_out
    first_norm, first_pull = jax.vjp(layer_norm, flat_tokens + attended, gain_one, shift_one)
    first_low = first_norm.astype(bf16)
    inner_pre = jnp.dot(first_low, in_full, preferred_element_type=f32) + bias_inner
    active, gelu_pull = jax.vjp(gelu_exact, inner_pre)
    active_low = active.astype(bf16)
    feed_out = jnp.dot(active_low, out_full, preferred_element_type=f32) + bias_feed
    output, second_pull = jax.vjp(layer_norm, first_norm + feed_out, gain_two, shift_two)
    local_start = lax.axis_index("seq") * block_size
    slot_ids = jnp.arange(positions.shape[1], dtype=jnp.int32)
    live_slots = slot_ids[None, :] < counts[:, None]
    block_places = jnp.arange(block_size, dtype=jnp.int32)
    hit_table = (
        (positions[:, :, None] - local_start == block_places[None, None, :])
        & live_slots[:, :, None]
    ).astype(f32)
    dense_grad = jnp.einsum(
        "smb,smd->sbd", hit_table, cotangent, precision=lax.Precision.HIGHEST
    ).reshape(token_rows, model_width)
    grad_sum_two, grad_gain_two, grad_shift_two = second_pull(dense_grad)
    feed_back = grad_sum_two.astype(bf16)
    grad_bias_feed = column_sum(feed_back)
    grad_out_matrix = jnp.einsum("rf,rd->fd", active_low, feed_back, preferred_element_type=f32)
    grad_active = jnp.einsum("rd,fd->rf", feed_back, out_full, preferred_element_type=f32)
    (grad_inner,) = gelu_pull(grad_active)
    inner_back = grad_inner.astype(bf16)
    grad_bias_inner = column_sum(inner_back)
    grad_in_matrix = jnp.einsum("rd,rf->df", first_low, inner_back, preferred_element_type=f32)
    grad_first = grad_sum_two + jnp.einsum(
        "rf,df->rd", inner_back, in_full, preferred_element_type=f32
    )
    grad_sum_one, grad_gain_one, grad_shift_one = first_pull(grad_first)
    attended_back = grad_sum_one.astype(bf16)
    grad_bias_out = column_sum(attended_back)
    grad_attn_out = jnp.einsum("rd,re->de", context_low, attended_back, preferred_element_type=f32)
    context_back = jnp.einsum(
        "re,de->rd", attended_back, attn_full[3], preferred_element_type=f32
    ).astype(bf16)
    context_back = context_back.reshape(sequences, block_size, head_count, head_size)
    grad_probs = jnp.einsum(
        "sqhe,skhe->shqk", context_back, value_heads, preferred_element_type=f32
    )
    row_delta = jnp.sum(attn_probs * grad_probs, -1, keepdims=True)
    scores_back = (attn_probs * (grad_probs - row_delta)).astype(bf16)
    query_back = (
        (
            jnp.einsum("shqk,skhe->sqhe", scores_back, key_heads, preferred_element_type=f32)
            * score_scale
        )
        .reshape(token_rows, model_width)
        .astype(bf16)
    )
    value_term = jnp.einsum("shqk,sqhe->skhe", probs_low, context_back, preferred_element_type=f32)
    key_term = (
        jnp.einsum("shqk,sqhe->skhe", scores_back, query_heads, preferred_element_type=f32)
        * score_scale
    )
    term_shape = (sequences, length, model_width)
    key_grads, value_grads = (
        lax.psum_scatter(
            key_term.reshape(term_shape).astype(jnp.bfloat16),
            "seq",
            scatter_dimension=1,
            tiled=True,
        ).astype(jnp.float32),
        lax.psum_scatter(
            value_term.reshape(term_shape).astype(jnp.bfloat16),
            "seq",
            scatter_dimension=1,
            tiled=True,
        ).astype(jnp.float32),
    )
    key_back = key_grads.reshape(token_rows, model_width).astype(bf16)
    value_back = value_grads.reshape(token_rows, model_width).astype(bf16)
    stacked_back = jnp.stack([query_back, key_back, value_back])
    grad_qkv = jnp.einsum("rd,kre->kde", flat_low, stacked_back, preferred_element_type=f32)
    grad_tokens = grad_sum_one + jnp.einsum(
        "kre,kde->rd", stacked_back, attn_full[:3], preferred_element_type=f32
    )
    grad_attn_all = jnp.concatenate([grad_qkv, grad_attn_out[None]], 0)
    grad_vector_all = jnp.concatenate(
        [
            column_sum(query_back),
            column_sum(value_back),
            grad_bias_out,
            grad_bias_feed,
            grad_gain_one,
            grad_shift_one,
            grad_gain_two,
            grad_shift_two,
            grad_bias_inner,
        ]
    )
    local_grads = (grad_attn_all, grad_in_matrix, grad_out_matrix, grad_vector_all)
    summed_whole = lax.psum(
        (local_grads[0], local_grads[1], local_grads[2], local_grads[3]), ("seq", "dp")
    )
    square_sum = sum((jnp.sum(total * total) for total in summed_whole))
    owner_index = lax.axis_index("seq") * lax.axis_size("dp") + lax.axis_index("dp")
    shares = (
        lax.dynamic_slice_in_dim(
            summed_whole[0], owner_index * attn_weights.shape[1], attn_weights.shape[1], 1
        ),
        lax.dynamic_slice_in_dim(
            summed_whole[1], owner_index * ffn_in.shape[0], ffn_in.shape[0], 0
        ),
        lax.dynamic_slice_in_dim(
            summed_whole[2], owner_index * ffn_out.shape[0], ffn_out.shape[0], 0
        ),
        lax.dynamic_slice_in_dim(
            summed_whole[3], owner_index * vectors.shape[0], vectors.shape[0], 0
        ),
    )
    grad_norm = jnp.sqrt(square_sum)
    clip_factor = 1.0 / jnp.maximum(grad_norm, 1.0)
    clipped = tuple((share * clip_factor for share in shares))
    params = (attn_weights, ffn_in, ffn_out, vectors)
    firsts = (attn_first, ffn_in_first, ffn_out_first, vector_first)
    seconds = (attn_second, ffn_in_second, ffn_out_second, vector_second)
    moved = [adam_direction(firsts[index], seconds[index], clipped[index]) for index in range(4)]
    directions = [moved[index][2] + weight_decay * params[index] for index in range(3)]
    weight_sq = jnp.concatenate(
        [
            jnp.sum(attn_weights * attn_weights, axis=(1, 2)),
            jnp.sum(ffn_in * ffn_in)[None],
            jnp.sum(ffn_out * ffn_out)[None],
        ]
    )
    dir_sq = jnp.concatenate(
        [
            jnp.sum(directions[0] * directions[0], axis=(1, 2)),
            jnp.sum(directions[1] * directions[1])[None],
            jnp.sum(directions[2] * directions[2])[None],
        ]
    )
    lamb_sq = lax.psum(jnp.stack([weight_sq, dir_sq]), ("seq", "dp"))
    lamb_norms = jnp.sqrt(lamb_sq)
    trust_ratio = lamb_norms[0] / lamb_norms[1]
    new_attn = attn_weights - step_rate * trust_ratio[:4, None, None] * directions[0]
    new_ffn_in = ffn_in - step_rate * trust_ratio[4] * directions[1]
    new_ffn_out = ffn_out - step_rate * trust_ratio[5] * directions[2]
    new_vectors = vectors - step_rate * moved[3][2]
    return (
        output.reshape(block_shape),
        grad_tokens.reshape(block_shape),
        clipped[0],
        clipped[1],
        clipped[2],
        clipped[3],
        moved[0][0],
        moved[1][0],
        moved[2][0],
        moved[3][0],
        moved[0][1],
        moved[1][1],
        moved[2][1],
        moved[3][1],
        new_attn,
        new_ffn_in,
        new_ffn_out,
        new_vectors,
        new_attn.astype(bf16),
        new_ffn_in.astype(bf16),
        new_ffn_out.astype(bf16),
        lamb_norms,
        trust_ratio,
        grad_norm,
    )


def solution(mesh):
    return jax.shard_map(
        body,
        mesh=mesh,
        in_specs=(
            P("dp", "seq", None),
            P("dp", None),
            P("dp"),
            P("dp", None, None),
            P(None, ("seq", "dp"), None),
            P(("seq", "dp"), None),
            P(("seq", "dp"), None),
            P(("seq", "dp")),
            P(None, ("seq", "dp"), None),
            P(("seq", "dp"), None),
            P(("seq", "dp"), None),
            P(("seq", "dp")),
            P(None, ("seq", "dp"), None),
            P(("seq", "dp"), None),
            P(("seq", "dp"), None),
            P(("seq", "dp")),
        ),
        out_specs=(
            P("dp", "seq", None),
            P("dp", "seq", None),
            P(None, ("seq", "dp"), None),
            P(("seq", "dp"), None),
            P(("seq", "dp"), None),
            P(("seq", "dp")),
            P(None, ("seq", "dp"), None),
            P(("seq", "dp"), None),
            P(("seq", "dp"), None),
            P(("seq", "dp")),
            P(None, ("seq", "dp"), None),
            P(("seq", "dp"), None),
            P(("seq", "dp"), None),
            P(("seq", "dp")),
            P(None, ("seq", "dp"), None),
            P(("seq", "dp"), None),
            P(("seq", "dp"), None),
            P(("seq", "dp")),
            P(None, ("seq", "dp"), None),
            P(("seq", "dp"), None),
            P(("seq", "dp"), None),
            P(),
            P(),
            P(),
        ),
        check_vma=False,
    )
```

profile of v0, /device:TPU:0, one launch (start us, length us, event | category | flops | bytes accessed | tf_op | source)
XLA Modules:
  0.0 1139.2 jit_solution(18235271576514705652)
XLA Ops:
  9.2 3.2 bitcast_convert_fusion
  12.4 65.6 %all-gather.6.cloned.1.call-done = bf16[4,768,768]{2,0,1:T(4,128)(2,1)} async-done(((bf16[4,24,768]{2,0,1:T(4,128)(2,1)}), bf16[4,768,768]{2,0,1:T(4,128)(2,1)}) %all-gather.6.cloned.1.call-update) | async-done | bytes 4718608 | tf_op jit(solution)/shard_map/all_gather | solution.py:67
  78.0 8.0 copy.161
  86.1 6.3 convolution_bitcast_fusion
  92.4 3.7 copy-done.10
  98.5 40.2 %all-reduce = bf16[9216]{0:T(1024)(128)(2,1)S(1)} all-reduce(bf16[9216]{0:T(1024)(128)(2,1)S(1)} %dynamic-update-slice), channel_id=1, replica_groups=mesh['seq'=4,'dp'=8] {'seq','dp'}, use_global_device_ids=true, to_apply=%add | all-reduce | flops 9216 | bytes 36864
  139.2 5.3 slice_bitcast_fusion
  145.4 3.1 fusion.20
  151.4 4.1 fusion.74
  156.2 7.4 slice.97
  163.7 4.2 all-gather.10.cloned.1.call-done
  167.9 7.7 copy.139
  175.6 15.8 %fusion.71 = (f32[8,12,128]{2,1,0:T(8,128)S(1)}, f32[8,12,128,512]{3,2,1,0:T(8,128)}) fusion(bf16[8,512,12,64]{1,3,2,0:T(8,128)(2,1)} %bitcast.142, f32[8,128,12,64]{1,0,3,2:T(8,128)S(1)} %bitcast.144, f32[12,64]{1,0:T(8,128)S(1)} %slice.76), kind=kOutput, calls=%fused_computation.163 | convolution fusion | flops 825754112 | bytes 34655232 | tf_op jit(solution)/shard_map/sub | solution.py:96
  191.4 48.4 %all-gather.8.cloned.1.call-done = bf16[8,512,768]{1,0,2:T(8,128)(2,1)} async-done(((bf16[8,128,768]{1,0,2:T(8,128)(2,1)}), bf16[8,512,768]{1,0,2:T(8,128)(2,1)}) %all-gather.8.cloned.1.call-update) | async-done | bytes 6291472 | tf_op jit(solution)/shard_map/all_gather | solution.py:86
  239.8 7.7 copy.137
  247.4 12.6 %fusion.33 = bf16[8,128,12,64]{1,3,2,0:T(8,128)(2,1)S(1)} fusion(bf16[8,512,12,64]{1,3,2,0:T(8,128)(2,1)} %bitcast.157, f32[8,12,128,512]{3,2,1,0:T(8,128)} %get-tuple-element.177, f32[8,12,128]{2,1,0:T(8,128)S(1)} %get-tuple-element.176), kind=kOutput, calls=%fused_computation.81 | convolution fusion | flops 818675712 | bytes 33079296 | tf_op jit(solution)/shard_map/shqk,skhe->sqhe/dot_general | solution.py:100
  261.3 4.8 fusion.72
  266.6 40.4 %all-gather.12.cloned.1.call-done = bf16[768,3072]{1,0:T(8,128)(2,1)} async-done(((bf16[24,3072]{1,0:T(8,128)(2,1)}), bf16[768,3072]{1,0:T(8,128)(2,1)}) %all-gather.12.cloned.1.call-update) | async-done | bytes 4718608 | tf_op jit(solution)/shard_map/all_gather | solution.py:68
  306.9 36.1 %multiply_convert_fusion.2 = (bf16[1024,3072]{1,0:T(8,128)(2,1)}, f32[1024,3072]{1,0:T(8,128)}, f32[1024,3072]{1,0:T(8,128)}) fusion(f32[3072]{0:T(1024)S(1)} %slice.101, bf16[768,3072]{1,0:T(8,128)(2,1)} %all-gather.12.cloned.1.call-done, f32[1024,768]{1,0:T(8,128)S(1)} %get-tuple-element.179, f32[768]{0:T(1024)S(1)} %get-tuple-element.170, ...), kind=kOutput, calls=%fused_computation.11 | convolution fusion | flops 5043388416 | bytes 39348224 | tf_op jit(solution)/shard_map/dot_general | solution.py:105
  343.0 29.9 %all-gather.14.cloned.1.call-done = bf16[3072,768]{1,0:T(8,128)(2,1)} async-done(((bf16[96,768]{1,0:T(8,128)(2,1)}), bf16[3072,768]{1,0:T(8,128)(2,1)}) %all-gather.14.cloned.1.call-update) | async-done | bytes 4718608 | tf_op jit(solution)/shard_map/all_gather | solution.py:69
  372.9 8.8 fusion.73
  385.2 3.0 fusion.67
  390.3 18.9 %convert_reduce_fusion = (f32[3072]{0:T(1024)}, bf16[1024,3072]{1,0:T(8,128)(2,1)}) fusion(f32[1024,3072]{1,0:T(8,128)} %get-tuple-element.162, bf16[1024,768]{1,0:T(8,128)(2,1)} %get-tuple-element.154, bf16[3072,768]{1,0:T(8,128)(2,1)} %all-gather.14.cloned.1.call-done, f32[1024,3072]{1,0:T(8,128)} %get-tuple-element.180, f32[3072]{0:T(1024)S(1)} %slice.101), kind=kOutput, calls=%fused_computation.8 | convolution fusion | flops 4885312512 | bytes 37773312 | tf_op jit(solution)/shard_map/rd,fd->rf/dot_general | solution.py:125
  409.2 10.1 multiply_reduce_fusion.5
  424.6 2.6 convolution_convert_fusion
  429.4 12.2 %fusion.17 = bf16[8,12,64,512]{3,2,1,0:T(8,128)(2,1)} fusion(bf16[8,128,12,64]{1,0,3,2:T(8,128)(2,1)S(1)} %bitcast.172, f32[8,12,128,512]{3,2,1,0:T(8,128)} %get-tuple-element.177, f32[8,12,128]{2,1,0:T(8,128)S(1)} %copy-done.31), kind=kOutput, calls=%fused_computation.40 | convolution fusion | flops 821035008 | bytes 33079296 | tf_op jit(solution)/shard_map/shqk,sqhe->skhe/dot_general | solution.py:154
  441.6 9.6 copy.157
  451.2 7.5 copy.170
  458.8 22.1 %multiply_reduce_fusion = (f32[8,12,128]{2,1,0:T(8,128)S(1)}, f32[8,12,128,512]{3,2,1,0:T(8,128)}) fusion(f32[8,12,128,512]{3,2,1,0:T(8,128)} %get-tuple-element.177, f32[8,12,128]{2,1,0:T(8,128)S(1)} %copy-done.31, bf16[8,512,12,64]{1,3,2,0:T(8,128)(2,1)} %bitcast.158, bf16[8,128,12,64]{1,0,3,2:T(8,128)(2,1)S(1)} %bitcast.173), kind=kOutput, calls=%fused_computation.2 | convolution fusion | flops 824168448 | bytes 58294272 | tf_op jit(solution)/shard_map/sqhe,skhe->shqk/dot_general | solution.py:141
  480.9 22.8 %multiply_convert_fusion = bf16[8,12,128,512]{3,2,1,0:T(8,128)(2,1)} fusion(f32[8,12,128,512]{3,2,1,0:T(8,128)} %get-tuple-element.185, f32[8,12,128]{2,1,0:T(8,128)S(1)} %get-tuple-element.184, f32[8,12,128,512]{3,2,1,0:T(8,128)} %get-tuple-element.177, f32[8,12,128]{2,1,0:T(8,128)S(1)} %copy-done.31), kind=kLoop, calls=%fused_computation.1 | loop fusion | flops 25165824 | bytes 63012864 | tf_op jit(solution)/shard_map/convert_element_type | solution.py:145
  503.7 10.2 multiply_convert_fusion.1
  513.9 9.3 copy.155
  523.2 7.5 copy.168
  530.9 10.8 convert_reduce_fusion.4
  545.4 5.0 convolution_bitcast_fusion.2
  550.4 10.8 fusion.55
  561.3 7.9 fusion.79
  572.4 28.7 %reduce-scatter.7.cloned.1.call-done = bf16[128,6144]{1,0:T(8,128)(2,1)} async-done(((bf16[512,6144]{1,0:T(8,128)(2,1)}), bf16[128,6144]{1,0:T(8,128)(2,1)}) %reduce-scatter.7.cloned.1.call-update) | async-done | bytes 1572880
  604.5 4.4 convolution_bitcast_fusion.1
  609.0 4.2 pad_maximum_fusion
  615.0 42.0 %psum.38 = f32[9216]{0:T(1024)S(1)} all-reduce(f32[9216]{0:T(1024)S(1)} %constant_dynamic-update-slice_fusion), channel_id=1, replica_groups=mesh['seq'=4,'dp'=8] {'seq','dp'}, use_global_device_ids=true, to_apply=%region_28.0 | all-reduce | flops 9216 | bytes 73728 | tf_op jit(solution)/shard_map/psum | solution.py:196
  657.6 388.0 %all-reduce.4.cloned.1.call-done = (f32[4,768,768]{2,1,0:T(8,128)}, f32[768,3072]{1,0:T(8,128)}, f32[3072,768]{1,0:T(8,128)}) async-done(((f32[4,768,768]{2,1,0:T(8,128)}, f32[768,3072]{1,0:T(8,128)}, f32[3072,768]{1,0:T(8,128)}), (f32[4,768,768]{2,1,0:T(8,128)}, f32[768,3072]{1,0:T(8,128)}, f32[3072,768]{1,0:T(8,128)})) %all-reduce.4.cloned.1.call-update) | async-done | bytes 28311568 | tf_op jit(solution)/shard_map/psum | solution.py:196
  1045.6 6.9 multiply_reduce_fusion.4
  1052.5 3.0 multiply_reduce_fusion.3
  1055.6 3.0 multiply_reduce_fusion.2
  1068.7 2.7 maximum_bitcast_fusion
  1071.4 10.0 bitcast_add_fusion.1
  1081.3 40.2 %psum.39 = f32[2,6]{1,0:T(2,128)S(1)} all-reduce(f32[2,6]{1,0:T(2,128)S(1)} %pad_maximum_fusion.6), channel_id=1, replica_groups=mesh['seq'=4,'dp'=8] {'seq','dp'}, use_global_device_ids=true, to_apply=%region_36.0 | all-reduce | flops 12 | bytes 96 | tf_op jit(solution)/shard_map/psum | solution.py:237
  (204 shorter events, 52.0 us)
Async XLA Ops:
  7.2 144.2 %copy-start = (f32[8,128,768]{2,1,0:T(8,128)S(1)}, f32[8,128,768]{2,1,0:T(8,128)}, u32[]{:S(2)}) copy-start(f32[8,128,768]{2,1,0:T(8,128)} %param.19) | copy-start | bytes 9437188
  7.2 70.8 %all-gather.6.cloned.1.call-start = ((), (), s32[]{:S(2)}) async-start(), calls=%async_computation.2 | async-start | bytes 4866048 | tf_op jit(solution)/shard_map/all_gather | solution.py:67
  9.2 158.7 %all-gather.10.cloned.1.call-start = ((), (), s32[]{:S(2)}) async-start(), calls=%async_computation.4 | async-start | bytes 7864320 | tf_op jit(solution)/shard_map/all_gather | solution.py:85
  92.4 3.7 copy-start.10
  98.1 141.7 %all-gather.8.cloned.1.call-start = ((), (), s32[]{:S(2)}) async-start(), calls=%async_computation.3 | async-start | bytes 7864320 | tf_op jit(solution)/shard_map/all_gather | solution.py:86
  139.2 233.7 %copy-start.34 = (f32[768]{0:T(1024)}, f32[768]{0:T(1024)S(1)}, u32[]{:S(2)}) copy-start(f32[768]{0:T(1024)S(1)} %get-tuple-element.170) | copy-start | bytes 9220
  145.3 5.9 copy-start.54
  145.4 6.0 copy-start.48
  148.5 158.5 %all-gather.12.cloned.1.call-start = ((), (), s32[]{:S(2)}) async-start(), calls=%async_computation.5 | async-start | bytes 4866048 | tf_op jit(solution)/shard_map/all_gather | solution.py:68
  149.2 223.7 %all-gather.14.cloned.1.call-start = ((), (), s32[]{:S(2)}) async-start(), calls=%async_computation.6 | async-start | bytes 4866048 | tf_op jit(solution)/shard_map/all_gather | solution.py:69
  150.9 418.2 %reduce-scatter.9.cloned.1.call-start = ((), (), s32[]{:S(2)}) async-start(), calls=%async_computation.8 | async-start | bytes 7864320
  151.4 24.2 %copy-start.32 = (f32[12,64]{1,0:T(8,128)}, f32[12,64]{1,0:T(8,128)S(1)}, u32[]{:S(2)}) copy-start(f32[12,64]{1,0:T(8,128)S(1)} %slice.76) | copy-start | bytes 9220
  151.4 4.1 copy-start.8
  156.2 19.4 %copy-start.2 = (f32[96,8,8,128]{3,2,1,0:T(8,128)}, f32[96,8,8,128]{3,2,1,0:T(8,128)S(1)}, u32[]{:S(2)}) copy-start(f32[96,8,8,128]{3,2,1,0:T(8,128)S(1)} %copy.164) | copy-start | bytes 9437188
  191.4 56.1 %copy-start.30 = (f32[8,12,128]{2,1,0:T(8,128)}, f32[8,12,128]{2,1,0:T(8,128)S(1)}, u32[]{:S(2)}) copy-start(f32[8,12,128]{2,1,0:T(8,128)S(1)} %get-tuple-element.176) | copy-start | bytes 147460
  261.3 4.8 copy-start.20
  266.0 153.3 %copy-start.4 = (f32[1024,768]{1,0:T(8,128)}, f32[1024,768]{1,0:T(8,128)S(1)}, u32[]{:S(2)}) copy-start(f32[1024,768]{1,0:T(8,128)S(1)} %get-tuple-element.179) | copy-start | bytes 9437188
  306.9 66.0 %copy-start.47 = (f32[768]{0:T(1024)S(1)}, f32[768]{0:T(1024)}, u32[]{:S(2)}) copy-start(f32[768]{0:T(1024)} %get-tuple-element.168) | copy-start | bytes 9220
  372.9 9.4 copy-start.36
  420.9 3.7 copy-start.16
  458.7 142.4 %reduce-scatter.7.cloned.1.call-start = ((), (), s32[]{:S(2)}) async-start(), calls=%async_computation.7 | async-start | bytes 7864320
  480.9 22.8 %copy-start.3 = (f32[96,8,8,128]{3,2,1,0:T(8,128)S(1)}, f32[96,8,8,128]{3,2,1,0:T(8,128)}, u32[]{:S(2)}) copy-start(f32[96,8,8,128]{3,2,1,0:T(8,128)} %copy-done.2) | copy-start | bytes 9437188
  480.9 22.8 %copy-start.33 = (f32[12,64]{1,0:T(8,128)S(1)}, f32[12,64]{1,0:T(8,128)}, u32[]{:S(2)}) copy-start(f32[12,64]{1,0:T(8,128)} %copy-done.32) | copy-start | bytes 9220
  530.7 514.9 %all-reduce.4.cloned.1.call-start = ((), (), s32[]{:S(2)}) async-start(), calls=%async_computation.9 | async-start | bytes 56623104 | tf_op jit(solution)/shard_map/psum | solution.py:196
  545.4 5.0 copy-start.5
  545.4 5.0 copy-start.35
  545.4 15.8 %slice-start.3 = ((s8[6291456]{0:T(1024)(128)(4,1)}), s8[4194304]{0:T(1024)(128)(4,1)S(1)}, s32[]{:S(2)}) async-start(s8[6291456]{0:T(1024)(128)(4,1)} %bitcast.175), calls=%async_computation.13 | async-start | bytes 8388608
  550.4 10.9 copy-start.22
  550.4 10.9 slice-start.4
  604.5 4.4 copy-start.15
  1045.6 6.9 copy-start.9
  1045.6 9.9 slice-start
  1045.6 9.9 slice-start.1
  1055.5 5.9 copy-start.11
  1055.5 5.9 copy-start.24
  1055.6 5.9 copy-start.25
  1055.6 8.0 copy-start.13
  1055.6 8.0 copy-start.26
  1055.6 8.0 copy-start.27
  1058.6 7.5 copy-start.14
  1058.6 7.5 copy-start.28
  1058.6 7.5 copy-start.29
  1058.6 12.7 %copy-start.39 = (f32[1024]{0:T(1024)S(1)}, f32[1024]{0:T(1024)}, u32[]{:S(2)}) copy-start(f32[1024]{0:T(1024)} %copy-done.38) | copy-start | bytes 12292
  1071.3 52.6 %copy-start.46 = (f32[288]{0:T(512)S(1)}, f32[288]{0:T(512)}, u32[]{:S(2)}) copy-start(f32[288]{0:T(512)} %param.23) | copy-start | bytes 3460
  1071.4 52.6 %copy-start.51 = (f32[288]{0:T(512)S(1)}, f32[288]{0:T(512)}, u32[]{:S(2)}) copy-start(f32[288]{0:T(512)} %param.31) | copy-start | bytes 3460
  1071.4 52.6 %copy-start.52 = (f32[288]{0:T(512)S(1)}, f32[288]{0:T(512)}, u32[]{:S(2)}) copy-start(f32[288]{0:T(512)} %param.27) | copy-start | bytes 3460
  1071.4 59.4 %copy-start.1 = (f32[8,128,768]{2,1,0:T(8,128)S(1)}, f32[8,128,768]{2,1,0:T(8,128)}, u32[]{:S(2)}) copy-start(f32[8,128,768]{2,1,0:T(8,128)} %param.19) | copy-start | bytes 9437188
  1121.5 9.3 copy-start.53
  (20 other events, 43.9 us)
Sparse Core Ops, SparseCore 0:
  11.6 66.3 all-gather.5
  98.2 69.6 all-gather.9
  169.7 70.0 all-gather.7
  243.2 63.6 all-gather.11
  310.4 62.4 all-gather.13
  458.9 69.0 reduce-scatter.8
  530.9 70.1 reduce-scatter.6
  613.3 432.2 all-reduce.3
where the time goes:
time: 1150 us; the launch traced here: 1140 us
  waiting for transfers between devices  605 us (53%)
  matrix products  213 us (19%)
  blocking collectives  122 us (11%)
  local copies, waits for them, and re-layouts  99.9 us (9%)
  other arithmetic  76.9 us (7%)
  between operations  20.6 us (2%)
    psum x1, waiting for transfers between devices, body(): lax.psum((local_grads[0], local_grads[1], local_grads[2], local_grads[3])...  388 us
    unnamed x145, local copies, waits for them, and re-layouts  67.4 us
    all_gather x1, waiting for transfers between devices, body(): lax.all_gather(attn_weights.astype(bf16), ('seq', 'dp'), axis=1, tiled=True)  65.6 us
    all_gather x1, waiting for transfers between devices, body(): lax.all_gather(value_low.reshape(block_shape), 'seq', axis=1, tiled=True)  48.4 us
    psum x1, blocking collectives, body(): lax.psum((local_grads[0], local_grads[1], local_grads[2], local_grads[3])...  42 us
    all_gather x1, waiting for transfers between devices, body(): lax.all_gather(ffn_in.astype(bf16), ('seq', 'dp'), axis=0, tiled=True)  40.4 us
    psum x1, blocking collectives, body(): lamb_sq = lax.psum(jnp.stack([weight_sq, dir_sq]), ('seq', 'dp'))  40.2 us
    unnamed x1, blocking collectives  40.2 us
  transfers between devices with their start and end apart: 8, of which 7 were waited for; matrix products, arithmetic and copies ran while one was open for 20% of the time, Pallas kernels for 0%

commit v1 on v0

v1 whole, which is shorter than its diff:
```python
import jax
import jax.numpy as jnp
from jax import lax
from jax.sharding import PartitionSpec as P

H = 12
HD = 64
STEP = 5


decay_rate = 0.5
step_rate = 0.3
weight_decay = 0.01
adam_eps = 1e-06
norm_eps = 1e-12


def layer_norm(hidden, gain_vec, shift_vec):
    center = hidden - jnp.mean(hidden, -1, keepdims=True)
    spread = jnp.mean(center * center, -1, keepdims=True)
    return center * lax.rsqrt(spread + norm_eps) * gain_vec + shift_vec


def gelu_exact(inputs):
    return jax.nn.gelu(inputs, approximate=False)


def column_sum(inputs):
    return jnp.sum(inputs.astype(jnp.float32), axis=0)


def adam_direction(first_old, second_old, clipped):
    first_new = decay_rate * first_old + (1.0 - decay_rate) * clipped
    second_new = decay_rate * second_old + (1.0 - decay_rate) * clipped * clipped
    correct = 1.0 - decay_rate**STEP
    direction = first_new / correct / (jnp.sqrt(second_new / correct) + adam_eps)
    return (first_new, second_new, direction)


def body(
    tokens,
    positions,
    counts,
    cotangent,
    attn_weights,
    ffn_in,
    ffn_out,
    vectors,
    attn_first,
    ffn_in_first,
    ffn_out_first,
    vector_first,
    attn_second,
    ffn_in_second,
    ffn_out_second,
    vector_second,
):
    bf16 = jnp.bfloat16
    f32 = jnp.float32
    sequences, block_size, model_width = tokens.shape
    head_count = H
    head_size = HD
    parts = lax.axis_size("seq")
    length = block_size * parts
    own = sequences // parts
    rows = own * length
    slots = positions.shape[1]
    score_scale = head_size ** (-0.5)
    attn_full = lax.all_gather(attn_weights.astype(bf16), ("seq", "dp"), axis=1, tiled=True)
    in_full = lax.all_gather(ffn_in.astype(bf16), ("seq", "dp"), axis=0, tiled=True)
    out_full = lax.all_gather(ffn_out.astype(bf16), ("seq", "dp"), axis=0, tiled=True)
    vec_full = lax.all_gather(vectors.astype(bf16), ("seq", "dp"), axis=0, tiled=True)
    vec_float = vec_full.astype(f32)
    pieces = [vec_float[index * model_width : (index + 1) * model_width] for index in range(8)]
    bias_query, bias_value, bias_out, bias_feed, gain_one, shift_one, gain_two, shift_two = pieces
    bias_inner = vec_float[8 * model_width :]
    token_high = tokens.astype(bf16)
    token_rest = (tokens - token_high.astype(f32)).astype(bf16)
    flat_low = lax.all_to_all(token_high, "seq", 0, 1, tiled=True).reshape(rows, model_width)
    flat_rest = lax.all_to_all(token_rest, "seq", 0, 1, tiled=True).reshape(rows, model_width)
    flat_tokens = flat_low.astype(f32) + flat_rest.astype(f32)
    first_own = lax.axis_index("seq") * own
    my_places = lax.dynamic_slice_in_dim(positions, first_own, own, 0)
    my_counts = lax.dynamic_slice_in_dim(counts, first_own, own, 0)
    my_cotangent = lax.dynamic_slice_in_dim(cotangent, first_own, own, 0)
    hit = my_places[:, :, None] == jnp.arange(length, dtype=jnp.int32)[None, None, :]
    hit_low = hit.astype(bf16)
    live = jnp.arange(slots, dtype=jnp.int32)[None, :] < my_counts[:, None]

    def pick(dense):
        return jnp.einsum(
            "sjl,sld->sjd",
            hit_low,
            dense.reshape(own, length, -1),
            preferred_element_type=f32,
        ).reshape(own * slots, -1)

    projected = jnp.einsum("rd,kde->kre", flat_low, attn_full[:3], preferred_element_type=f32)
    query_low = (projected[0] + bias_query).astype(bf16)
    key_low = projected[1].astype(bf16)
    value_low = (projected[2] + bias_value).astype(bf16)
    query_heads = query_low.reshape(own, length, head_count, head_size)
    key_heads = key_low.reshape(own, length, head_count, head_size)
    value_heads = value_low.reshape(own, length, head_count, head_size)

    def softmax_of(query_part):
        scores = (
            jnp.einsum("sqhe,skhe->shqk", query_part, key_heads, preferred_element_type=f32)
            * score_scale
        )
        exponent = jnp.exp(scores - jnp.max(scores, -1, keepdims=True))
        return exponent / jnp.sum(exponent, -1, keepdims=True)

    probs_all = softmax_of(query_heads).astype(bf16)
    context = jnp.einsum("shqk,skhe->sqhe", probs_all, value_heads, preferred_element_type=f32)
    context_low = context.reshape(rows, model_width).astype(bf16)

    def front(token_part, context_part):
        attended = jnp.dot(context_part, attn_full[3], preferred_element_type=f32) + bias_out
        return layer_norm(token_part + attended, gain_one, shift_one)

    def inner_of(low):
        return jnp.dot(low, in_full, preferred_element_type=f32) + bias_inner

    def feed_of(active):
        return jnp.dot(active.astype(bf16), out_full, preferred_element_type=f32) + bias_feed

    norm_all = front(flat_tokens, context_low)
    feed_all = feed_of(gelu_exact(inner_of(norm_all.astype(bf16))))
    output = layer_norm(norm_all + feed_all, gain_two, shift_two)
    output = lax.all_to_all(
        output.astype(bf16).reshape(own, length, model_width), "seq", 1, 0, tiled=True
    ).astype(f32)

    context_slot = pick(context_low).astype(bf16)
    token_slot = pick(flat_low) + pick(flat_rest)
    attended = jnp.dot(context_slot, attn_full[3], preferred_element_type=f32) + bias_out
    first_norm, first_pull = jax.vjp(layer_norm, token_slot + attended, gain_one, shift_one)
    first_low = first_norm.astype(bf16)
    active, gelu_pull = jax.vjp(gelu_exact, inner_of(first_low))
    active_low = active.astype(bf16)
    feed_out = feed_of(active)
    _, second_pull = jax.vjp(layer_norm, first_norm + feed_out, gain_two, shift_two)
    slot_grad = jnp.where(live[:, :, None], my_cotangent, 0.0).reshape(own * slots, model_width)
    grad_sum_two, grad_gain_two, grad_shift_two = second_pull(slot_grad)
    feed_back = grad_sum_two.astype(bf16)
    grad_bias_feed = column_sum(feed_back)
    grad_out_matrix = jnp.einsum("rf,rd->fd", active_low, feed_back, preferred_element_type=f32)
    grad_active = jnp.einsum("rd,fd->rf", feed_back, out_full, preferred_element_type=f32)
    (grad_inner,) = gelu_pull(grad_active)
    inner_back = grad_inner.astype(bf16)
    grad_bias_inner = column_sum(inner_back)
    grad_in_matrix = jnp.einsum("rd,rf->df", first_low, inner_back, preferred_element_type=f32)
    grad_first = grad_sum_two + jnp.einsum(
        "rf,df->rd", inner_back, in_full, preferred_element_type=f32
    )
    grad_sum_one, grad_gain_one, grad_shift_one = first_pull(grad_first)
    attended_back = grad_sum_one.astype(bf16)
    grad_bias_out = column_sum(attended_back)
    grad_attn_out = jnp.einsum(
        "rd,re->de", context_slot, attended_back, preferred_element_type=f32
    )
    context_back = jnp.einsum(
        "re,de->rd", attended_back, attn_full[3], preferred_element_type=f32
    ).astype(bf16)
    context_back = context_back.reshape(own, slots, head_count, head_size)
    query_slot = pick(query_low).astype(bf16).reshape(own, slots, head_count, head_size)
    attn_probs = softmax_of(query_slot)
    probs_low = attn_probs.astype(bf16)
    grad_probs = jnp.einsum(
        "sqhe,skhe->shqk", context_back, value_heads, preferred_element_type=f32
    )
    row_delta = jnp.sum(attn_probs * grad_probs, -1, keepdims=True)
    scores_back = (attn_probs * (grad_probs - row_delta)).astype(bf16)
    query_back = (
        (
            jnp.einsum("shqk,skhe->sqhe", scores_back, key_heads, preferred_element_type=f32)
            * score_scale
        )
        .reshape(own * slots, model_width)
        .astype(bf16)
    )
    value_back = jnp.einsum("shqk,sqhe->skhe", probs_low, context_back, preferred_element_type=f32)
    value_back = value_back.astype(bf16).reshape(rows, model_width)
    key_back = (
        jnp.einsum("shqk,sqhe->skhe", scores_back, query_slot, preferred_element_type=f32)
        * score_scale
    )
    key_back = key_back.astype(bf16).reshape(rows, model_width)
    token_slot_low = pick(flat_low).astype(bf16)
    grad_qkv = jnp.stack(
        [
            jnp.einsum("rd,re->de", token_slot_low, query_back, preferred_element_type=f32),
            jnp.einsum("rd,re->de", flat_low, key_back, preferred_element_type=f32),
            jnp.einsum("rd,re->de", flat_low, value_back, preferred_element_type=f32),
        ]
    )
    slot_tokens = grad_sum_one + jnp.einsum(
        "re,de->rd", query_back, attn_full[0], preferred_element_type=f32
    )
    slot_high = slot_tokens.astype(bf16)
    slot_rest = (slot_tokens - slot_high.astype(f32)).astype(bf16)

    def spread(part):
        return jnp.einsum(
            "sjl,sjd->sld",
            hit_low,
            part.reshape(own, slots, model_width),
            preferred_element_type=f32,
        )

    grad_tokens = (
        spread(slot_high)
        + spread(slot_rest)
        + (
            jnp.einsum("re,de->rd", key_back, attn_full[1], preferred_element_type=f32)
            + jnp.einsum("re,de->rd", value_back, attn_full[2], preferred_element_type=f32)
        ).reshape(own, length, model_width)
    )
    grad_tokens = lax.all_to_all(
        grad_tokens.astype(bf16), "seq", 1, 0, tiled=True
    ).astype(f32)
    grad_attn_all = jnp.concatenate([grad_qkv, grad_attn_out[None]], 0)
    grad_vector_all = jnp.concatenate(
        [
            column_sum(query_back),
            column_sum(value_back),
            grad_bias_out,
            grad_bias_feed,
            grad_gain_one,
            grad_shift_one,
            grad_gain_two,
            grad_shift_two,
            grad_bias_inner,
        ]
    )

    def scatter(part, axis):
        return lax.psum_scatter(
            part.astype(bf16), ("seq", "dp"), scatter_dimension=axis, tiled=True
        ).astype(f32)

    shares = (
        scatter(grad_attn_all, 1),
        scatter(grad_in_matrix, 0),
        scatter(grad_out_matrix, 0),
        scatter(grad_vector_all, 0),
    )
    square_sum = lax.psum(sum((jnp.sum(total * total) for total in shares)), ("seq", "dp"))
    grad_norm = jnp.sqrt(square_sum)
    clip_factor = 1.0 / jnp.maximum(grad_norm, 1.0)
    clipped = tuple((share * clip_factor for share in shares))
    params = (attn_weights, ffn_in, ffn_out, vectors)
    firsts = (attn_first, ffn_in_first, ffn_out_first, vector_first)
    seconds = (attn_second, ffn_in_second, ffn_out_second, vector_second)
    moved = [adam_direction(firsts[index], seconds[index], clipped[index]) for index in range(4)]
    directions = [moved[index][2] + weight_decay * params[index] for index in range(3)]
    weight_sq = jnp.concatenate(
        [
            jnp.sum(attn_weights * attn_weights, axis=(1, 2)),
            jnp.sum(ffn_in * ffn_in)[None],
            jnp.sum(ffn_out * ffn_out)[None],
        ]
    )
    dir_sq = jnp.concatenate(
        [
            jnp.sum(directions[0] * directions[0], axis=(1, 2)),
            jnp.sum(directions[1] * directions[1])[None],
            jnp.sum(directions[2] * directions[2])[None],
        ]
    )
    lamb_sq = lax.psum(jnp.stack([weight_sq, dir_sq]), ("seq", "dp"))
    lamb_norms = jnp.sqrt(lamb_sq)
    trust_ratio = lamb_norms[0] / lamb_norms[1]
    new_attn = attn_weights - step_rate * trust_ratio[:4, None, None] * directions[0]
    new_ffn_in = ffn_in - step_rate * trust_ratio[4] * directions[1]
    new_ffn_out = ffn_out - step_rate * trust_ratio[5] * directions[2]
    new_vectors = vectors - step_rate * moved[3][2]
    return (
        output,
        grad_tokens,
        clipped[0],
        clipped[1],
        clipped[2],
        clipped[3],
        moved[0][0],
        moved[1][0],
        moved[2][0],
        moved[3][0],
        moved[0][1],
        moved[1][1],
        moved[2][1],
        moved[3][1],
        new_attn,
        new_ffn_in,
        new_ffn_out,
        new_vectors,
        new_attn.astype(bf16),
        new_ffn_in.astype(bf16),
        new_ffn_out.astype(bf16),
        lamb_norms,
        trust_ratio,
        grad_norm,
    )


def solution(mesh):
    return jax.shard_map(
        body,
        mesh=mesh,
        in_specs=(
            P("dp", "seq", None),
            P("dp", None),
            P("dp"),
            P("dp", None, None),
            P(None, ("seq", "dp"), None),
            P(("seq", "dp"), None),
            P(("seq", "dp"), None),
            P(("seq", "dp")),
            P(None, ("seq", "dp"), None),
            P(("seq", "dp"), None),
            P(("seq", "dp"), None),
            P(("seq", "dp")),
            P(None, ("seq", "dp"), None),
            P(("seq", "dp"), None),
            P(("seq", "dp"), None),
            P(("seq", "dp")),
        ),
        out_specs=(
            P("dp", "seq", None),
            P("dp", "seq", None),
            P(None, ("seq", "dp"), None),
            P(("seq", "dp"), None),
            P(("seq", "dp"), None),
            P(("seq", "dp")),
            P(None, ("seq", "dp"), None),
            P(("seq", "dp"), None),
            P(("seq", "dp"), None),
            P(("seq", "dp")),
            P(None, ("seq", "dp"), None),
            P(("seq", "dp"), None),
            P(("seq", "dp"), None),
            P(("seq", "dp")),
            P(None, ("seq", "dp"), None),
            P(("seq", "dp"), None),
            P(("seq", "dp"), None),
            P(("seq", "dp")),
            P(None, ("seq", "dp"), None),
            P(("seq", "dp"), None),
            P(("seq", "dp"), None),
            P(),
            P(),
            P(),
        ),
        check_vma=False,
    )
```

time: 1150 us -> 747 us (0.65)
  waiting for transfers between devices: 605 us -> 206 us
  blocking collectives: 122 us -> 213 us
  matrix products: 213 us -> 160 us
  other arithmetic: 76.9 us -> 47.3 us
  local copies, waits for them, and re-layouts: 99.9 us -> 78.9 us
    psum x1 -> x0, waiting for transfers between devices: 388 us -> none  [body(): lax.psum((local_grads[0], local_grads[1], local_grads[2], local_grads[3])...]
    reduce_scatter x0 -> x2, waiting for transfers between devices: none -> 187 us  [scatter(): lax.psum_scatter(part.astype(bf16), ('seq', 'dp'), scatter_dimension=axis...]
    unnamed x1 -> x2, blocking collectives: 40.2 us -> 108 us
    all_gather x1, waiting for transfers between devices: 65.6 us -> 0.01 us  [body(): lax.all_gather(attn_weights.astype(bf16), ('seq', 'dp'), axis=1, tiled=True)]
    all_gather x2 -> x0, waiting for transfers between devices: 52.6 us -> none  [the longest x1 48.4 us: body(): lax.all_gather(value_low.reshape(block_shape), 'seq', axis=1, tiled=True)]
    unnamed x145 -> x177, local copies, waits for them, and re-layouts: 67.4 us -> 24.9 us
    all_gather x1, waiting for transfers between devices: 40.4 us -> 0.01 us  [body(): lax.all_gather(ffn_in.astype(bf16), ('seq', 'dp'), axis=0, tiled=True)]
    unnamed x10 -> x7, waiting for transfers between devices: 28.9 us -> 0.12 us
  transfers between devices with their start and end apart: 8 -> 9, of which waited for: 7 -> 4; matrix products, arithmetic and copies ran while one was open for 20% -> 26% of each run, Pallas kernels for 0% -> 0%
where the time goes in v1:
time: 747 us; the launch traced here: 738 us
  blocking collectives  213 us (29%)
  waiting for transfers between devices  206 us (28%)
  matrix products  160 us (21%)
  local copies, waits for them, and re-layouts  78.9 us (11%)
  other arithmetic  47.3 us (6%)
  between operations  21.6 us (3%)
  starting transfers between devices  11.2 us (1%)
    reduce_scatter x2, waiting for transfers between devices, scatter(): lax.psum_scatter(part.astype(bf16), ('seq', 'dp'), scatter_dimension=axis...  187 us
    unnamed x2, blocking collectives  108 us
    dot_general x2, matrix products, inner_of(): return jnp.dot(low, in_full, preferred_element_type=f32) + bias_inner  55.8 us
    psum x1, blocking collectives, body(): lax.psum(sum((jnp.sum(total * total) for total in shares)), ('seq', 'dp'))  40 us
    psum x1, blocking collectives, body(): lamb_sq = lax.psum(jnp.stack([weight_sq, dir_sq]), ('seq', 'dp'))  39.4 us
    all_to_all x1, blocking collectives, body(): lax.all_to_all(token_high, 'seq', 0, 1, tiled=True)  26 us
    unnamed x177, local copies, waits for them, and re-layouts  24.9 us
    sub x1, matrix products, softmax_of(): exponent = jnp.exp(scores - jnp.max(scores, -1, keepdims=True))  15.7 us
  transfers between devices with their start and end apart: 9, of which 4 were waited for; matrix products, arithmetic and copies ran while one was open for 26% of the time, Pallas kernels for 0%

profile of v1, /device:TPU:0, one launch (start us, length us, event | category | flops | bytes accessed | tf_op | source)
XLA Modules:
  0.0 738.0 jit_solution(8190164027097660765)
XLA Ops:
  10.7 4.6 subtract_convert_fusion
  15.3 26.0 %all_to_all.54 = bf16[8,128,768]{2,1,0:T(8,128)(2,1)} all-to-all(bf16[8,128,768]{2,1,0:T(8,128)(2,1)S(1)} %get-tuple-element.71), channel_id=1, replica_groups=mesh['seq'=4,'dp'=8] {'seq'}, dimensions={0} | all-to-all | bytes 3145728 | tf_op jit(solution)/shard_map/all_to_all | solution.py:79
  41.3 3.6 all-to-all-start.1
  46.0 56.5 %all-reduce = bf16[9216]{0:T(1024)(128)(2,1)S(1)} all-reduce(bf16[9216]{0:T(1024)(128)(2,1)S(1)} %dynamic-update-slice), channel_id=1, replica_groups=mesh['seq'=4,'dp'=8] {'seq','dp'}, use_global_device_ids=true, to_apply=%add | all-reduce | flops 9216 | bytes 36864
  105.3 2.7 fusion.167
  112.7 6.1 fusion.28
  122.5 3.7 squeeze.28
  126.2 2.3 copy.162
  128.5 2.9 convert_element_type.237
  131.4 6.2 squeeze.27
  137.6 2.3 fusion.73
  140.2 15.7 %fusion.177 = (f32[2,12,512]{2,1,0:T(8,128)}, f32[2,12,512,512]{2,3,1,0:T(8,128)}) fusion(bf16[2,512,12,64]{1,0,3,2:T(2,128)(2,1)S(1)} %convert_element_type.237, f32[2,512,12,64]{1,0,3,2:T(2,128)} %squeeze.28, f32[12,64]{1,0:T(8,128)S(1)} %copy-done.54), kind=kOutput, calls=%fused_computation.264 | convolution fusion | flops 825754112 | bytes 29936640 | tf_op jit(solution)/shard_map/sub | solution.py:111
  156.0 13.2 %fusion.49 = bf16[2,12,64,512]{3,2,1,0:T(8,128)(2,1)} fusion(f32[2,12,512,512]{2,3,1,0:T(8,128)} %get-tuple-element.89, f32[2,12,512]{2,1,0:T(8,128)} %get-tuple-element.88, f32[2,512,12,64]{1,0,3,2:T(2,128)} %squeeze.27, f32[12,64]{1,0:T(8,128)} %slice.91), kind=kOutput, calls=%fused_computation.84 | convolution fusion | flops 820248576 | bytes 29936640 | tf_op jit(solution)/shard_map/shqk,skhe->sqhe/dot_general | solution.py:115
  171.3 8.0 %fusion.174 = (bf16[1,768,768]{2,0,1:T(2,128)(2,1)}, bf16[1,768,768]{2,0,1:T(2,128)(2,1)S(1)}, bf16[1,768,768]{2,0,1:T(2,128)(2,1)}, bf16[1,768,768]{2,0,1:T(2,128)(2,1)}) fusion(bf16[4,768,768]{2,0,1:T(4,128)(2,1)S(1)} %bitcast.184), kind=kLoop, calls=%fused_computation.261 | loop fusion | bytes 9437184 | tf_op jit(solution)/shard_map/slice | solution.py:199
  182.5 2.6 copy-done.2
  185.2 3.9 fusion.192
  189.0 20.1 %multiply_convert_fusion.2 = (bf16[256,3072]{1,0:T(8,128)(2,1)}, f32[256,3072]{1,0:T(8,128)}, f32[256,3072]{1,0:T(8,128)}) fusion(f32[3072]{0:T(1024)S(1)} %copy-done.47, bf16[768,3072]{1,0:T(8,128)(2,1)} %all-gather.6.cloned.1.call-done, f32[256,768]{1,0:T(8,128)S(1)} %get-tuple-element.95, f32[768]{0:T(1024)S(1)} %get-tuple-element.81, ...), kind=kOutput, calls=%fused_computation.61 | convolution fusion | flops 1260847104 | bytes 13389824 | tf_op jit(solution)/shard_map/dot_general | solution.py:123
  209.2 6.4 all-gather.8.cloned.1.call-done
  215.6 4.5 fusion.191
  222.4 2.8 fusion.166
  225.2 2.3 multiply_reduce_fusion.5
  235.2 12.2 %fusion.195 = (bf16[12,64]{1,0:T(8,128)(2,1)}, bf16[2,512,12,64]{1,3,2,0:T(8,128)(2,1)}) fusion(f32[2,12,128]{2,1,0:T(8,128)S(1)} %get-tuple-element.100, f32[2,12,128,512]{3,2,1,0:T(8,128)} %copy-done.2, bf16[2,128,12,64]{1,0,3,2:T(2,128)(2,1)} %reshape.288), kind=kOutput, calls=%fused_computation.272 | convolution fusion | flops 210766592 | bytes 8271360 | tf_op jit(solution)/shard_map/shqk,sqhe->skhe/dot_general | solution.py:183
  247.4 6.5 multiply_reduce_fusion.1
  267.3 3.6 copy.163
  270.9 3.2 copy.174
  274.2 5.2 convolution_convert_fusion.1
  279.5 3.2 copy.128
  287.7 3.7 convolution_convert_fusion
  293.3 35.6 %fusion.45.clone.4 = bf16[1024,3072]{1,0:T(8,128)(2,1)S(1)} fusion(f32[3072]{0:T(1024)S(1)} %copy-done.48, bf16[768,3072]{1,0:T(8,128)(2,1)} %all-gather.6.cloned.1.call-done, f32[1024,768]{1,0:T(8,128)S(1)} %copy-done.21, f32[768]{0:T(1024)S(1)} %get-tuple-element.81, f32[768]{0:T(1024)S(1)} %get-tuple-element.80, ...), kind=kOutput, calls=%fused_computation.9.clone.clone.clone.clone.clone.clone.1 | convolution fusion | flops 5043388416 | bytes 14182400 | tf_op jit(solution)/shard_map/dot_general | solution.py:123
  329.0 5.4 fusion.187
  335.7 2.8 copy.130
  338.4 3.8 all-to-all-start.2
  342.3 2.4 subtract_convert_fusion.1
  344.7 3.1 fusion.75
  351.4 2.8 copy.150
  354.2 12.2 %all-to-all-done.2 = bf16[2,512,768]{2,0,1:T(2,128)(2,1)S(1)} async-done(((bf16[2,512,768]{2,0,1:T(2,128)(2,1)}), bf16[2,512,768]{2,0,1:T(2,128)(2,1)S(1)}, u32[]{:S(2)}, u32[]{:S(2)}) %all-to-all-start.2) | async-done | bytes 1572896 | tf_op jit(solution)/shard_map/all_to_all | solution.py:131
  366.4 3.6 all-to-all-start.3
  371.8 51.3 %all-reduce.1 = bf16[9216]{0:T(1024)(128)(2,1)S(1)} all-reduce(bf16[9216]{0:T(1024)(128)(2,1)S(1)} %constant_dynamic-update-slice_fusion), channel_id=5, replica_groups=mesh['seq'=4,'dp'=8] {'seq','dp'}, use_global_device_ids=true, to_apply=%region_32.33.clone | all-reduce | flops 9216 | bytes 36864
  423.8 2.7 convert_bitcast_fusion.1
  427.7 2.5 convert_bitcast_fusion
  431.3 79.1 %reduce-scatter.6.cloned.1.call-done = bf16[24,3072]{1,0:T(8,128)(2,1)} async-done(((bf16[768,3072]{1,0:T(8,128)(2,1)}), bf16[24,3072]{1,0:T(8,128)(2,1)}) %reduce-scatter.6.cloned.1.call-update) | async-done | bytes 147472 | tf_op jit(solution)/shard_map/reduce_scatter | solution.py:239
  514.0 107.8 %reduce-scatter.8.cloned.1.call-done = bf16[96,768]{1,0:T(8,128)(2,1)} async-done(((bf16[3072,768]{1,0:T(8,128)(2,1)}), bf16[96,768]{1,0:T(8,128)(2,1)}) %reduce-scatter.8.cloned.1.call-update) | async-done | bytes 147472 | tf_op jit(solution)/shard_map/reduce_scatter | solution.py:239
  624.7 3.9 copy.131
  628.6 40.0 %psum.14 = f32[]{:T(128)} all-reduce(f32[]{:T(128)S(6)} %add.293), channel_id=1, replica_groups=mesh['seq'=4,'dp'=8] {'seq','dp'}, use_global_device_ids=true, to_apply=%region_34.35 | all-reduce | flops 1 | bytes 8 | tf_op jit(solution)/shard_map/psum | solution.py:249
  669.4 2.3 multiply_reduce_fusion.15
  671.7 2.8 multiply_reduce_fusion.14
  676.1 2.7 maximum_bitcast_fusion
  680.8 39.4 %psum.15 = f32[2,6]{1,0:T(2,128)S(1)} all-reduce(f32[2,6]{1,0:T(2,128)S(1)} %pad_maximum_fusion.1), channel_id=1, replica_groups=mesh['seq'=4,'dp'=8] {'seq','dp'}, use_global_device_ids=true, to_apply=%region_41.42 | all-reduce | flops 12 | bytes 96 | tf_op jit(solution)/shard_map/psum | solution.py:272
  (275 shorter events, 76.1 us)
Async XLA Ops:
  7.2 98.0 %copy-start = (s32[8,128]{1,0:T(8,128)S(1)}, s32[8,128]{1,0:T(8,128)}, u32[]{:S(2)}) copy-start(s32[8,128]{1,0:T(8,128)} %param.17) | copy-start | bytes 12292
  7.2 105.5 %all-gather.4.cloned.1.call-start = ((), (), s32[]{:S(2)}) async-start(), calls=%async_computation.7 | async-start | bytes 4866048 | tf_op jit(solution)/shard_map/all_gather | solution.py:69
  9.0 180.0 %all-gather.6.cloned.1.call-start = ((), (), s32[]{:S(2)}) async-start(), calls=%async_computation.8 | async-start | bytes 4866048 | tf_op jit(solution)/shard_map/all_gather | solution.py:70
  15.3 29.6 %copy-start.26 = (f32[96,768]{1,0:T(8,128)S(1)}, f32[96,768]{1,0:T(8,128)}, u32[]{:S(2)}) copy-start(f32[96,768]{1,0:T(8,128)} %param.22) | copy-start | bytes 884740
  15.3 30.4 %copy-start.55 = (f32[288]{0:T(512)S(1)}, f32[288]{0:T(512)}, u32[]{:S(2)}) copy-start(f32[288]{0:T(512)} %param.23) | copy-start | bytes 3460
  15.3 89.7 %copy-start.69 = (s32[8]{0:T(128)S(1)}, s32[8]{0:T(128)}, u32[]{:S(2)}) copy-start(s32[8]{0:T(128)} %param.18) | copy-start | bytes 100
  41.3 68.2 %all-to-all-start.1 = ((bf16[8,128,768]{2,1,0:T(8,128)(2,1)}), bf16[8,128,768]{2,1,0:T(8,128)(2,1)S(1)}, u32[]{:S(2)}, u32[]{:S(2)}) async-start(bf16[8,128,768]{2,1,0:T(8,128)(2,1)} %get-tuple-element.70), calls=%async_computation.1 | async-start | bytes 3145728 | tf_op jit(solution)/shard_map/all_to_all | solution.py:80
  44.9 170.7 %all-gather.8.cloned.1.call-start = ((), (), s32[]{:S(2)}) async-start(), calls=%async_computation.9 | async-start | bytes 4866048 | tf_op jit(solution)/shard_map/all_gather | solution.py:71
  45.7 384.6 %reduce-scatter.10.cloned.1.call-start = ((), (), s32[]{:S(2)}) async-start(), calls=%async_computation.12 | async-start | bytes 4866048
  103.8 111.9 %copy-start.58 = (f32[768]{0:T(1024)}, f32[768]{0:T(1024)S(1)}, u32[]{:S(2)}) copy-start(f32[768]{0:T(1024)S(1)} %get-tuple-element.82) | copy-start | bytes 9220
  103.8 117.5 %copy-start.41 = (f32[768]{0:T(1024)}, f32[768]{0:T(1024)S(1)}, u32[]{:S(2)}) copy-start(f32[768]{0:T(1024)S(1)} %get-tuple-element.78) | copy-start | bytes 9220
  105.2 64.0 %copy-start.43 = (s32[2,128]{1,0:T(2,128)}, s32[2,128]{1,0:T(2,128)S(1)}, u32[]{:S(2)}) copy-start(s32[2,128]{1,0:T(2,128)S(1)} %constant_dynamic-slice_fusion) | copy-start | bytes 3076
  131.4 8.8 %copy-start.3 = (bf16[2,512,12,64]{1,0,3,2:T(2,128)(2,1)}, bf16[2,512,12,64]{1,0,3,2:T(2,128)(2,1)S(1)}, u32[]{:S(2)}) copy-start(bf16[2,512,12,64]{1,0,3,2:T(2,128)(2,1)S(1)} %convert_element_type.237) | copy-start | bytes 4718596
  156.0 15.3 %slice-start.2 = ((s8[4718592]{0:T(1024)(128)(4,1)}), s8[4194304]{0:T(1024)(128)(4,1)S(1)}, s32[]{:S(2)}) async-start(s8[4718592]{0:T(1024)(128)(4,1)} %bitcast.183), calls=%async_computation.15 | async-start | bytes 8388608
  156.0 15.3 %slice-start.3 = ((s8[4718592]{0:T(1024)(128)(4,1)}), s8[524288]{0:T(1024)(128)(4,1)S(1)}, s32[]{:S(2)}) async-start(s8[4718592]{0:T(1024)(128)(4,1)} %bitcast.183), calls=%async_computation.16 | async-start | bytes 1048576
  171.2 8.0 %copy-start.18 = (bf16[2,128,768]{2,1,0:T(8,128)(2,1)}, bf16[2,128,768]{2,1,0:T(8,128)(2,1)S(1)}, u32[]{:S(2)}) copy-start(bf16[2,128,768]{2,1,0:T(8,128)(2,1)S(1)} %convolution_convert_fusion.6) | copy-start | bytes 1179652
  171.3 8.0 %copy-start.24 = (f32[2,128,768]{2,1,0:T(8,128)S(1)}, f32[2,128,768]{2,1,0:T(8,128)}, u32[]{:S(2)}) copy-start(f32[2,128,768]{2,1,0:T(8,128)} %convolution_add_fusion.4) | copy-start | bytes 2359300
  215.6 6.8 slice-start.6
  215.6 6.8 slice-start.7
  215.6 6.8 copy-start.71
  227.8 7.4 %copy-start.61 = (f32[256]{0:T(256)}, f32[256]{0:T(256)S(1)}, u32[]{:S(2)}) copy-start(f32[256]{0:T(256)S(1)} %negate_multiply_fusion.2) | copy-start | bytes 3076
  235.2 12.2 %copy-start.53 = (f32[12,64]{1,0:T(8,128)S(1)}, f32[12,64]{1,0:T(8,128)}, u32[]{:S(2)}) copy-start(f32[12,64]{1,0:T(8,128)} %slice.91) | copy-start | bytes 9220
  247.4 6.5 slice-start.1
  274.2 236.2 %reduce-scatter.6.cloned.1.call-start = ((), (), s32[]{:S(2)}) async-start(), calls=%async_computation.10 | async-start | bytes 4866048 | tf_op jit(solution)/shard_map/reduce_scatter | solution.py:239
  279.4 342.4 %reduce-scatter.8.cloned.1.call-start = ((), (), s32[]{:S(2)}) async-start(), calls=%async_computation.11 | async-start | bytes 4866048 | tf_op jit(solution)/shard_map/reduce_scatter | solution.py:239
  293.3 35.6 %copy-start.59 = (f32[768]{0:T(1024)S(1)}, f32[768]{0:T(1024)}, u32[]{:S(2)}) copy-start(f32[768]{0:T(1024)} %copy-done.58) | copy-start | bytes 9220
  293.3 35.7 %copy-start.68 = (bf16[3072,768]{1,0:T(8,128)(2,1)S(1)}, bf16[3072,768]{1,0:T(8,128)(2,1)}, u32[]{:S(2)}) copy-start(bf16[3072,768]{1,0:T(8,128)(2,1)} %all-gather.8.cloned.1.call-done) | copy-start | bytes 14155780
  335.7 6.6 copy-start.23
  335.7 6.6 copy-start.33
  335.7 6.6 copy-start.62
  338.4 27.9 %all-to-all-start.2 = ((bf16[2,512,768]{2,0,1:T(2,128)(2,1)}), bf16[2,512,768]{2,0,1:T(2,128)(2,1)S(1)}, u32[]{:S(2)}, u32[]{:S(2)}) async-start(bf16[2,512,768]{2,0,1:T(2,128)(2,1)} %copy.130), calls=%async_computation.2 | async-start | bytes 3145728 | tf_op jit(solution)/shard_map/all_to_all | solution.py:131
  351.3 18.7 %copy-start.46 = (bf16[12,64]{1,0:T(8,128)(2,1)S(1)}, bf16[12,64]{1,0:T(8,128)(2,1)}, u32[]{:S(2)}) copy-start(bf16[12,64]{1,0:T(8,128)(2,1)} %get-tuple-element.106) | copy-start | bytes 4612
  351.3 18.7 %copy-start.60 = (bf16[12,64]{1,0:T(8,128)(2,1)S(1)}, bf16[12,64]{1,0:T(8,128)(2,1)}, u32[]{:S(2)}) copy-start(bf16[12,64]{1,0:T(8,128)(2,1)} %get-tuple-element.108) | copy-start | bytes 4612
  351.3 19.2 %copy-start.52 = (bf16[768]{0:T(1024)(128)(2,1)S(1)}, bf16[768]{0:T(1024)(128)(2,1)}, u32[]{:S(2)}) copy-start(bf16[768]{0:T(1024)(128)(2,1)} %get-tuple-element.60) | copy-start | bytes 4612
  351.4 19.4 %copy-start.51 = (bf16[768]{0:T(1024)(128)(2,1)S(1)}, bf16[768]{0:T(1024)(128)(2,1)}, u32[]{:S(2)}) copy-start(bf16[768]{0:T(1024)(128)(2,1)} %get-tuple-element.58) | copy-start | bytes 4612
  351.4 19.6 %copy-start.64 = (bf16[768]{0:T(1024)(128)(2,1)S(1)}, bf16[768]{0:T(1024)(128)(2,1)}, u32[]{:S(2)}) copy-start(bf16[768]{0:T(1024)(128)(2,1)} %get-tuple-element.26) | copy-start | bytes 4612
  351.4 19.8 %copy-start.63 = (bf16[768]{0:T(1024)(128)(2,1)S(1)}, bf16[768]{0:T(1024)(128)(2,1)}, u32[]{:S(2)}) copy-start(bf16[768]{0:T(1024)(128)(2,1)} %get-tuple-element.28) | copy-start | bytes 4612
  351.4 20.0 %copy-start.50 = (bf16[768]{0:T(1024)(128)(2,1)S(1)}, bf16[768]{0:T(1024)(128)(2,1)}, u32[]{:S(2)}) copy-start(bf16[768]{0:T(1024)(128)(2,1)} %get-tuple-element.24) | copy-start | bytes 4612
  351.4 20.2 %copy-start.49 = (bf16[768]{0:T(1024)(128)(2,1)S(1)}, bf16[768]{0:T(1024)(128)(2,1)}, u32[]{:S(2)}) copy-start(bf16[768]{0:T(1024)(128)(2,1)} %get-tuple-element.56) | copy-start | bytes 4612
  351.4 20.4 %copy-start.57 = (bf16[3072]{0:T(1024)(128)(2,1)S(1)}, bf16[3072]{0:T(1024)(128)(2,1)}, u32[]{:S(2)}) copy-start(bf16[3072]{0:T(1024)(128)(2,1)} %get-tuple-element.54) | copy-start | bytes 18436
  366.4 60.2 %all-to-all-start.3 = ((bf16[2,512,768]{2,0,1:T(2,128)(2,1)}), bf16[2,512,768]{2,0,1:T(2,128)(2,1)S(1)}, u32[]{:S(2)}, u32[]{:S(2)}) async-start(bf16[2,512,768]{2,0,1:T(2,128)(2,1)} %copy.150), calls=%async_computation.3 | async-start | bytes 3145728 | tf_op jit(solution)/shard_map/all_to_all | solution.py:220
  431.3 192.8 %copy-start.37 = (bf16[24,4,768]{2,1,0:T(4,128)(2,1)}, bf16[24,4,768]{2,1,0:T(4,128)(2,1)S(1)}, u32[]{:S(2)}) copy-start(bf16[24,4,768]{2,1,0:T(4,128)(2,1)S(1)} %reshape.303) | copy-start | bytes 442372
  624.7 44.7 %copy-start.25 = (f32[4,24,768]{2,1,0:T(8,128)S(1)}, f32[4,24,768]{2,1,0:T(8,128)}, u32[]{:S(2)}) copy-start(f32[4,24,768]{2,1,0:T(8,128)} %param.20) | copy-start | bytes 884740
  678.8 43.9 %copy-start.56 = (f32[288]{0:T(512)S(1)}, f32[288]{0:T(512)}, u32[]{:S(2)}) copy-start(f32[288]{0:T(512)} %param.23) | copy-start | bytes 3460
  678.8 43.9 %copy-start.65 = (f32[288]{0:T(512)S(1)}, f32[288]{0:T(512)}, u32[]{:S(2)}) copy-start(f32[288]{0:T(512)} %param.31) | copy-start | bytes 3460
  678.8 43.9 %copy-start.66 = (f32[288]{0:T(512)S(1)}, f32[288]{0:T(512)}, u32[]{:S(2)}) copy-start(f32[288]{0:T(512)} %param.27) | copy-start | bytes 3460
  678.8 50.7 %copy-start.1 = (s32[8,128]{1,0:T(8,128)S(1)}, s32[8,128]{1,0:T(8,128)}, u32[]{:S(2)}) copy-start(s32[8,128]{1,0:T(8,128)} %param.17) | copy-start | bytes 12292
  720.2 9.3 %copy-start.67 = (f32[2,6]{1,0:T(2,128)}, f32[2,6]{1,0:T(2,128)S(1)}, u32[]{:S(2)}) copy-start(f32[2,6]{1,0:T(2,128)S(1)} %sqrt.22) | copy-start | bytes 148
  (41 other events, 112.4 us)
Sparse Core Ops, SparseCore 0:
  11.6 71.5 all-gather.3
  86.8 62.6 all-gather.5
  153.1 62.4 all-gather.7
  274.3 118.3 reduce-scatter.9
  398.9 111.4 reduce-scatter.5
  515.7 106.0 reduce-scatter.7

commit v2 on v1

--- a/solution.py
+++ b/solution.py
@@ -1,18 +1,659 @@
+import functools
 import jax
 import jax.numpy as jnp
 from jax import lax
 from jax.sharding import PartitionSpec as P
+from jax.experimental import pallas as pl
+from jax.experimental.pallas import tpu as pltpu
 
 H = 12
 HD = 64
 STEP = 5
-
 
 decay_rate = 0.5
 step_rate = 0.3
 weight_decay = 0.01
 adam_eps = 1e-06
 norm_eps = 1e-12
+f32 = jnp.float32
+bf16 = jnp.bfloat16
+MESH = pl.DeviceIdType.MESH
+
+
+class Place:
+    def __init__(self, mesh, shard_rows):
+        self.seq = mesh.shape["seq"]
+        self.dp = mesh.shape["dp"]
+        self.merge = 2
+        while (self.merge * shard_rows) % 16:
+            self.merge *= 2
+        self.seq_bits = self.seq.bit_length() - 1
+        self.far_bits = (self.dp // self.merge).bit_length() - 1
+        self.bits = self.seq_bits + self.far_bits
+        self.groups = self.seq * self.dp // self.merge
+        self.devices = self.seq * self.dp
+
+    def here(self):
+        self.s = lax.axis_index("seq")
+        self.d = lax.axis_index("dp")
+        self.member = lax.rem(self.d, self.merge)
+        self.core = lax.rem(self.d, 2)
+        self.weight = []
+        self.bit = []
+        for dim in range(self.bits):
+            if dim < self.seq_bits:
+                w = 1 << (self.seq_bits - 1 - dim)
+                self.bit.append(lax.rem(self.s // w, 2))
+            else:
+                w = self.merge << (self.bits - 1 - dim)
+                self.bit.append(lax.rem(self.d // w, 2))
+            self.weight.append(w)
+
+    def across(self, dim):
+        flip = self.weight[dim] * (1 - 2 * self.bit[dim])
+        if dim < self.seq_bits:
+            return (self.s + flip, self.d)
+        return (self.s, self.d + flip)
+
+    def other_core(self):
+        return (self.s, self.d + 1 - 2 * self.core)
+
+    def mates(self):
+        base = self.d - self.member
+        return [
+            (self.s, base + lax.rem(self.member + k, self.merge)) for k in range(1, self.merge)
+        ]
+
+    def row_mates(self):
+        return [(lax.rem(self.s + k, self.seq), self.d) for k in range(1, self.seq)]
+
+    def greet(self):
+        barrier = pltpu.get_barrier_semaphore()
+        everyone = self.mates() + self.row_mates()
+        everyone += [self.across(dim) for dim in range(self.seq_bits, self.bits)]
+        for device in everyone:
+            pl.semaphore_signal(barrier, inc=1, device_id=device, device_id_type=MESH)
+        pl.semaphore_wait(barrier, len(everyone))
+
+    def box(self, free):
+        return tuple(slice(None) if dim in free else self.bit[dim] for dim in range(self.bits))
+
+
+def erf(x):
+    x = jnp.clip(x, -3.832506856900711, 3.832506856900711)
+    x2 = x * x
+    top = jnp.float32(0.00022905065861350646)
+    for c in (
+        0.0034082910107109506,
+        0.050955695062380861,
+        0.18520832239976145,
+        1.128379143519084,
+    ):
+        top = top * x2 + jnp.float32(c)
+    low = jnp.float32(-1.1791602954361697e-7)
+    for c in (
+        0.000023547966471313185,
+        0.0010179625278914885,
+        0.014070470171167667,
+        0.11098505178285362,
+        0.49746925110067538,
+        1.0,
+    ):
+        low = low * x2 + jnp.float32(c)
+    return x * top / low
+
+
+def dot(a, b):
+    return jnp.dot(a, b, preferred_element_type=f32)
+
+
+def dot_t(a, b):
+    return lax.dot_general(a, b, (((1,), (1,)), ((), ())), preferred_element_type=f32)
+
+
+def t_dot(a, b):
+    return lax.dot_general(a, b, (((0,), (0,)), ((), ())), preferred_element_type=f32)
+
+
+def normalize(x):
+    center = x - jnp.mean(x, -1, keepdims=True)
+    inverse = lax.rsqrt(jnp.mean(center * center, -1, keepdims=True) + norm_eps)
+    return center * inverse, inverse
+
+
+class Flows:
+    def __init__(self, place, chunks, send, recv):
+        self.place = place
+        self.chunks = chunks
+        self.send = send
+        self.recv = recv
+        self.stages = place.bits
+
+    def number(self, chunk, part, stage):
+        return (chunk * 3 + part) * (self.stages + 1) + stage
+
+
+class Gather(Flows):
+    def copy(self, chunk, part, stage):
+        place = self.place
+        buf, rows, columns, order = self.chunks[chunk].part(part, place)
+        n = self.number(chunk, part, stage)
+        box = place.box(order[:stage]) + (rows, columns)
+        return pltpu.make_async_remote_copy(
+            src_ref=buf.at[box],
+            dst_ref=buf.at[box],
+            send_sem=self.send.at[n],
+            recv_sem=self.recv.at[n],
+            device_id=place.across(order[stage]),
+            device_id_type=MESH,
+        )
+
+    def hand(self, chunk):
+        place = self.place
+        buf, rows, columns = self.chunks[chunk].half(place)
+        n = self.number(chunk, 0, self.stages)
+        box = tuple(slice(None) for _ in range(place.bits)) + (rows, columns)
+        return pltpu.make_async_remote_copy(
+            src_ref=buf.at[box],
+            dst_ref=buf.at[box],
+            send_sem=self.send.at[n],
+            recv_sem=self.recv.at[n],
+            device_id=place.other_core(),
+            device_id_type=MESH,
+        )
+
+    def step(self, t):
+        for chunk in range(len(self.chunks)):
+            stage = t - chunk
+            if 0 <= stage <= self.stages:
+                for part in range(3):
+                    if stage > 0:
+                        self.copy(chunk, part, stage - 1).wait_recv()
+                    if stage < self.stages:
+                        self.copy(chunk, part, stage).start()
+                if stage == self.stages:
+                    self.hand(chunk).start()
+            if stage == self.stages + 1:
+                self.hand(chunk).wait_recv()
+
+    def last_step(self, chunk):
+        return chunk + self.stages + 1
+
+    def finish(self):
+        for chunk in range(len(self.chunks)):
+            for part in range(3):
+                for stage in range(self.stages):
+                    self.copy(chunk, part, stage).wait_send()
+            self.hand(chunk).wait_send()
+
+
+class Chunk:
+    def __init__(self, buf, first, width, orders, cuts=None):
+        self.buf, self.first, self.width, self.orders, self.cuts = buf, first, width, orders, cuts
+
+    def half(self, place):
+        half = self.width // 2
+        start = pl.multiple_of(self.first + place.core * half, 128)
+        return self.buf, slice(None), pl.ds(start, half)
+
+    def part(self, part, place):
+        half = self.width // 2
+        if self.cuts is None:
+            third = half // 3
+            start = pl.multiple_of(self.first + place.core * half + part * third, 128)
+            return self.buf, slice(None), pl.ds(start, third), self.orders[part]
+        start = pl.multiple_of(self.first + place.core * half, 128)
+        rows = pl.ds(self.cuts[part], self.cuts[part + 1] - self.cuts[part])
+        return self.buf, rows, pl.ds(start, half), self.orders[part]
+
+
+def weight_chunks(place, attn, first_ffn, second_ffn, reverse):
+    seq = list(range(place.seq_bits))
+    far = list(range(place.seq_bits, place.bits))[::-1]
+    left = far + seq[::-1]
+    right = far + seq
+    chunks = []
+
+    def orders(index):
+        a, b = (seq, seq[::-1]) if index % 2 else (seq[::-1], seq)
+        if index % 4 < 2:
+            third = a + far
+        else:
+            third = a[:1] + far + a[1:]
+        out = [left, right, third]
+        return [order[::-1] for order in out] if reverse else out
+
+    width = attn.shape[-1]
+    for m in range(4):
+        chunks.append(Chunk(attn.at[m], 0, width, orders(m)))
+    for j in range(first_ffn.shape[-1] // width):
+        chunks.append(Chunk(first_ffn, j * width, width, orders(j)))
+    rows = second_ffn.shape[-2]
+    third = rows // 3 // 16 * 16
+    for j in range(3):
+        chunks.append(
+            Chunk(second_ffn, j * width // 3, width // 3, orders(j), (0, third, 2 * third, rows))
+        )
+    return chunks
+
+
+def forward_kernel(
+    place,
+    vec_rows,
+    vec_count,
+    tokens_ref,
+    places_ref,
+    attn_ref,
+    in_ref,
+    out_ref,
+    vec_ref,
+    attn_hbm,
+    in_hbm,
+    out_hbm,
+    vec_hbm,
+    high_hbm,
+    query_hbm,
+    key_hbm,
+    value_hbm,
+    norm_hbm,
+    active_hbm,
+    slot_low_hbm,
+    slot_hbm,
+    slot_active_hbm,
+    slot_slope_hbm,
+    attn_buf,
+    in_buf,
+    out_buf,
+    vec_buf,
+    vec_acc,
+    vec,
+    attn_in,
+    in_in,
+    out_in,
+    joined,
+    send_high,
+    send_rest,
+    high,
+    rest,
+    query,
+    key,
+    value,
+    norm,
+    active,
+    slot_low,
+    slot,
+    slot_active,
+    slot_slope,
+    flow_send,
+    flow_recv,
+    mate_send,
+    mate_recv,
+    local_sem,
+    token_send,
+    token_recv,
+    vec_send,
+    vec_recv,
+    save_sem,
+):
+    place.here()
+    place.greet()
+    merge, seq = place.merge, place.seq
+    width = tokens_ref.shape[-1]
+    block = tokens_ref.shape[1]
+    own = tokens_ref.shape[0] // seq
+    length = block * seq
+    rows = own * length
+    slots = places_ref.shape[1]
+    mine = place.box(())
+
+    sources = (attn_ref, in_ref, out_ref)
+    stages = (attn_in, in_in, out_in)
+    mate_copies = []
+    for index in range(3):
+        for k, device in enumerate(place.mates()):
+            n = index * (merge - 1) + k
+            copy = pltpu.make_async_remote_copy(
+                src_ref=sources[index],
+                dst_ref=stages[index].at[place.member],
+                send_sem=mate_send.at[n],
+                recv_sem=mate_recv.at[n],
+                device_id=device,
+                device_id_type=MESH,
+            )
+            copy.start()
+            mate_copies.append(copy)
+    local = []
+    for index in range(3):
+        copy = pltpu.make_async_copy(
+            sources[index], stages[index].at[place.member], local_sem.at[index]
+        )
+        copy.start()
+        local.append(copy)
+    vec_mates = []
+    vec_buf.at[mine][place.member] = vec_ref[...]
+    for k, device in enumerate(place.mates()):
+        copy = pltpu.make_async_remote_copy(
+            src_ref=vec_ref,
+            dst_ref=vec_buf.at[mine].at[place.member],
+            send_sem=vec_send.at[k],
+            recv_sem=vec_recv.at[k],
+            device_id=device,
+            device_id_type=MESH,
+        )
+        copy.start()
+        vec_mates.append(copy)
+
+    def split(i, _):
+        x = tokens_ref[i]
+        top = x.astype(bf16)
+        send_high[i] = top
+        send_rest[i] = (x - top.astype(f32)).astype(bf16)
+        return 0
+
+    lax.fori_loop(0, own * seq, split, 0)
+    token_copies = []
+    my_columns = pl.ds(pl.multiple_of(place.s * block, block), block)
+    for half, (source, target) in enumerate(((send_high, high), (send_rest, rest))):
+        for k, device in enumerate(place.row_mates()):
+            n = half * (seq - 1) + k
+            token_copies.append(
+                pltpu.make_async_remote_copy(
+                    src_ref=source.at[pl.ds(device[0] * own, own)],
+                    dst_ref=target.at[:, my_columns],
+                    send_sem=token_send.at[n],
+                    recv_sem=token_recv.at[n],
+                    device_id=device,
+                    device_id_type=MESH,
+                )
+            )
+        target.at[:, my_columns][...] = source[pl.ds(place.s * own, own)]
+    for copy in token_copies[: seq - 1]:
+        copy.start()
+
+    flows = Gather(place, weight_chunks(place, attn_buf, in_buf, out_buf, False), flow_send, flow_recv)
+
+    def join(chunks, part):
+        count = part.shape[1]
+        for i in range(merge):
+            joined[i * count : (i + 1) * count, : part.shape[-1]] = part[i]
+        for chunk in chunks:
+            buf, _, columns = chunk.half(place)
+            buf.at[mine + (slice(None), columns)][...] = joined[: merge * count, columns].astype(bf16)
+
+    for k in range(3):
+        local[k].wait()
+        for copy in mate_copies[k * (merge - 1) : (k + 1) * (merge - 1)]:
+            copy.wait_recv()
+        if k == 0:
+            for m in range(4):
+                join(flows.chunks[m : m + 1], attn_in.at[:, m])
+        elif k == 1:
+            join(flows.chunks[4:-3], in_in)
+        else:
+            join(flows.chunks[-3:], out_in)
+
+    def vec_copy(stage):
+        order = list(range(place.bits))
+        box = place.box(order[:stage])
+        return pltpu.make_async_remote_copy(
+            src_ref=vec_buf.at[box],
+            dst_ref=vec_buf.at[box],
+            send_sem=vec_send.at[merge - 1 + stage],
+            recv_sem=vec_recv.at[merge - 1 + stage],
+            device_id=place.across(order[stage]),
+            device_id_type=MESH,
+        )
+
+    for copy in vec_mates:
+        copy.wait_recv()
+    vec_copy(0).start()
+    flows.step(0)
+    for t in range(1, flows.stages + 1):
+        vec_copy(t - 1).wait_recv()
+        if t < flows.stages:
+            vec_copy(t).start()
+        flows.step(t)
+    for copy in token_copies[seq - 1 :]:
+        copy.start()
+
+    vec_acc[...] = jnp.zeros_like(vec_acc)
+    for owner in range(place.devices):
+        group, member = divmod(owner, merge)
+        bits = tuple((group >> (place.bits - 1 - dim)) & 1 for dim in range(place.bits))
+        first, shift = divmod(vec_count * owner, 128)
+        count = (shift + vec_count + 127) // 128
+        vec_acc[first : first + count] += vec_buf.at[bits][member, :count]
+    per = width // 128
+    vec_acc[...] = vec_acc[...].astype(bf16).astype(f32)
+    for row in range(vec_rows):
+        vec[row : row + 1] = jnp.concatenate(
+            [vec_acc[row * per + k : row * per + k + 1] for k in range(per)], axis=1
+        )
+    saves = []
+
+    def save(source, target):
+        copy = pltpu.make_async_copy(source, target, save_sem.at[len(saves)])
+        copy.start()
+        saves.append(copy)
+
+    save(vec, vec_hbm)
+
+    for copy in token_copies[: seq - 1]:
+        copy.wait_recv()
+    tile = min(256, length)
+    per_seq = length // tile
+    save(high, high_hbm)
+    scale = HD**-0.5
+
+    for m, target in enumerate((query, key, value)):
+        flows.step(flows.last_step(m))
+        matrix = attn_buf.at[m].reshape(width, width)
+
+        def project(i, _):
+            sequence, at = i // per_seq, pl.ds(pl.multiple_of(lax.rem(i, per_seq) * tile, tile), tile)
+            result = dot(high[sequence, at], matrix[...])
+            if m == 0:
+                result = (result + vec[0:1]).astype(bf16) * scale
+            elif m == 2:
+                result = result + vec[1:2]
+            target[sequence, at] = result.astype(bf16)
+            return 0
+
+        lax.fori_loop(0, own * per_seq, project, 0)
+        save(target, (query_hbm, key_hbm, value_hbm)[m])
+
+    context = send_high.reshape(own, length, width)
+    for copy in token_copies[: seq - 1]:
+        copy.wait_send()
+    pairs = width // 128
+    turns = own * pairs
+    lane = lax.broadcasted_iota(jnp.int32, (1, 128), 1)
+
+    def attend(i, _):
+        for k in range(3):
+            @pl.when(i == (k + 1) * turns // 4)
+            def _():
+                flows.step(flows.last_step(3 + k))
+
+        sequence, pair = i // pairs, lax.rem(i, pairs)
+        at = pl.ds(pl.multiple_of(pair * 128, 128), 128)
+        keys, values = key[sequence, :, at], value[sequence, :, at]
+        for q in range(per_seq):
+            places = slice(q * tile, (q + 1) * tile)
+            queries = query[sequence, places, at]
+            heads = []
+            for head in range(2):
+                picked = jnp.where(lane // HD == head, queries, jnp.zeros_like(queries))
+                scores = dot_t(picked, keys)
+                exponent = jnp.exp(scores - jnp.max(scores, -1, keepdims=True))
+                total = jnp.sum(exponent, -1, keepdims=True)
+                heads.append(dot(exponent.astype(bf16), values) / total)
+            context[sequence, places, at] = jnp.where(lane < HD, heads[0], heads[1]).astype(bf16)
+        return 0
+
+    lax.fori_loop(0, turns, attend, 0)
+    flows.step(flows.last_step(6))
+
+    for copy in token_copies[seq - 1 :]:
+        copy.wait_recv()
+    out_matrix = attn_buf.at[3].reshape(width, width)
+
+    def front(i, _):
+        sequence, at = i // per_seq, pl.ds(pl.multiple_of(lax.rem(i, per_seq) * tile, tile), tile)
+        x = high[sequence, at].astype(f32) + rest[sequence, at].astype(f32)
+        x = x + (dot(context[sequence, at], out_matrix[...]) + vec[2:3])
+        x, _ = normalize(x)
+        norm[sequence, at] = x * vec[4:5] + vec[5:6]
+        return 0
+
+    lax.fori_loop(0, own * per_seq, front, 0)
+    save(norm, norm_hbm)
+
+    place_ids = lax.broadcasted_iota(jnp.int32, (length, slots), 0)
+    for sequence in range(own):
+        at = pl.ds(sequence * slots, slots)
+        hits = places_ref[pl.ds(place.s * own + sequence, 1)] == place_ids
+        hits = jnp.where(hits, 1.0, 0.0).astype(bf16)
+        slot_high = t_dot(hits, high[sequence])
+        slot_low[0, at] = slot_high.astype(bf16)
+        slot_context = t_dot(hits, context[sequence]).astype(bf16)
+        slot_low[1, at] = slot_context
+        slot_low[2, at] = t_dot(hits, query[sequence]).astype(bf16)
+        slot[0, at] = slot_high
+        slot[1, at] = t_dot(hits, rest[sequence])
+        x = slot[0, at] + slot[1, at]
+        x = x + (dot(slot_context, out_matrix[...]) + vec[2:3])
+        x, inverse = normalize(x)
+        slot[0, at] = x
+        slot[2, at] = jnp.broadcast_to(inverse, x.shape)
+        x = x * vec[4:5] + vec[5:6]
+        slot[1, at] = x
+        slot_low[3, at] = x.astype(bf16)
+    save(slot_low, slot_low_hbm)
+    save(slot, slot_hbm)
+    save(attn_buf, attn_hbm)
+
+    in_matrix = in_buf.reshape(width, in_buf.shape[-1])
+    for j in range(in_buf.shape[-1] // width):
+        if j > 0:
+            flows.step(flows.last_step(6 + j))
+        at = pl.ds(j * width, width)
+        bias = vec[8 + j : 9 + j]
+
+        def hidden(i, _):
+            sequence, here = i // per_seq, pl.ds(pl.multiple_of(lax.rem(i, per_seq) * tile, tile), tile)
+            x = dot(norm[sequence, here].astype(bf16), in_matrix[:, at]) + bias
+            active[sequence, here, at] = (0.5 * x * (1.0 + erf(x * 0.5**0.5))).astype(bf16)
+            return 0
+
+        lax.fori_loop(0, own * per_seq, hidden, 0)
+        x = dot(slot_low[3], in_matrix[:, at]) + bias
+        half = 0.5 * (1.0 + erf(x * 0.5**0.5))
+        slot_active[:, at] = (x * half).astype(bf16)
+        slot_slope[:, at] = half + x * jnp.exp(-0.5 * x * x) * 0.3989422804014327
+    save(active, active_hbm)
+    save(slot_active, slot_active_hbm)
+    save(slot_slope, slot_slope_hbm)
+    save(in_buf, in_hbm)
+    for t in range(flows.last_step(9) + 1, flows.last_step(len(flows.chunks) - 1) + 1):
+        flows.step(t)
+    save(out_buf, out_hbm)
+    flows.finish()
+    for copy in mate_copies + vec_mates + token_copies[seq - 1 :]:
+        copy.wait_send()
+    for stage in range(flows.stages):
+        vec_copy(stage).wait_send()
+    for copy in saves:
+        copy.wait()
+
+
+def forward_call(mesh, tokens, positions, attn_weights, ffn_in, ffn_out, vectors):
+    place = Place(mesh, ffn_in.shape[0])
+    sequences, block, width = tokens.shape
+    inner = ffn_in.shape[1]
+    slots = positions.shape[1]
+    own = sequences // place.seq
+    length = block * place.seq
+    vec_count = vectors.shape[0]
+    vec_rows = vec_count * place.devices // width
+    owner = lax.axis_index("seq") * place.dp + lax.axis_index("dp")
+    padded = lax.dynamic_update_slice_in_dim(
+        jnp.zeros((1024,), f32), vectors.astype(bf16).astype(f32), lax.rem(vec_count * owner, 128), 0
+    ).reshape(8, 128)
+    bits = (2,) * place.bits
+    r = ffn_in.shape[0]
+    joint = r * place.merge
+    joint_out = ffn_out.shape[0] * place.merge
+    flow_count = (4 + inner // width + 3) * 3 * (place.bits + 1)
+    attn_shape = (4,) + bits + (joint, width)
+    in_shape = bits + (joint, inner)
+    out_shape = bits + (joint_out, width)
+    seq_shape = (own, length, width)
+    rows = own * slots
+    results = [
+        (attn_shape, bf16),
+        (in_shape, bf16),
+        (out_shape, bf16),
+        ((16, width), f32),
+        (seq_shape, bf16),
+        (seq_shape, bf16),
+        (seq_shape, bf16),
+        (seq_shape, bf16),
+        (seq_shape, f32),
+        ((own, length, inner), bf16),
+        ((4, rows, width), bf16),
+        ((3, rows, width), f32),
+        ((rows, inner), bf16),
+        ((rows, inner), f32),
+    ]
+    vmem = pl.BlockSpec(memory_space=pltpu.VMEM)
+    hbm = pl.BlockSpec(memory_space=pl.ANY)
+    dma = pltpu.SemaphoreType.DMA
+    mates = place.merge - 1
+    return pl.pallas_call(
+        functools.partial(forward_kernel, place, vec_rows, vec_count),
+        out_shape=[jax.ShapeDtypeStruct(*one) for one in results],
+        in_specs=[vmem, vmem, hbm, hbm, hbm, vmem],
+        out_specs=[hbm] * len(results),
+        scratch_shapes=[
+            pltpu.VMEM(attn_shape, bf16),
+            pltpu.VMEM(in_shape, bf16),
+            pltpu.VMEM(out_shape, bf16),
+            pltpu.VMEM(bits + (place.merge, 8, 128), f32),
+            pltpu.VMEM((vec_rows * width // 128 + 8, 128), f32),
+            pltpu.VMEM((16, width), f32),
+            pltpu.VMEM((place.merge,) + attn_weights.shape, f32),
+            pltpu.VMEM((place.merge,) + ffn_in.shape, f32),
+            pltpu.VMEM((place.merge,) + ffn_out.shape, f32),
+            pltpu.VMEM((joint_out, inner), f32),
+            pltpu.VMEM((sequences, block, width), bf16),
+            pltpu.VMEM((sequences, block, width), bf16),
+            pltpu.VMEM(seq_shape, bf16),
+            pltpu.VMEM(seq_shape, bf16),
+            pltpu.VMEM(seq_shape, bf16),
+            pltpu.VMEM(seq_shape, bf16),
+            pltpu.VMEM(seq_shape, bf16),
+            pltpu.VMEM(seq_shape, f32),
+            pltpu.VMEM((own, length, inner), bf16),
+            pltpu.VMEM((4, rows, width), bf16),
+            pltpu.VMEM((3, rows, width), f32),
+            pltpu.VMEM((rows, inner), bf16),
+            pltpu.VMEM((rows, inner), f32),
+            dma((flow_count,)),
+            dma((flow_count,)),
+            dma((3 * mates,)),
+            dma((3 * mates,)),
+            dma((3,)),
+            dma((2 * (place.seq - 1),)),
+            dma((2 * (place.seq - 1),)),
+            dma((mates + place.bits,)),
+            dma((mates + place.bits,)),
+            dma((len(results),)),
+        ],
+        compiler_params=pltpu.CompilerParams(
+            collective_id=0, has_side_effects=True, vmem_limit_bytes=64 * 2**20 - 2**18
+        ),
+    )(tokens, positions, attn_weights, ffn_in, ffn_out, padded)
 
 
 def layer_norm(hidden, gain_vec, shift_vec):
@@ -38,6 +679,7 @@
 
 
 def body(
+    mesh,
     tokens,
     positions,
     counts,
@@ -66,19 +708,20 @@
     rows = own * length
     slots = positions.shape[1]
     score_scale = head_size ** (-0.5)
-    attn_full = lax.all_gather(attn_weights.astype(bf16), ("seq", "dp"), axis=1, tiled=True)
-    in_full = lax.all_gather(ffn_in.astype(bf16), ("seq", "dp"), axis=0, tiled=True)
-    out_full = lax.all_gather(ffn_out.astype(bf16), ("seq", "dp"), axis=0, tiled=True)
-    vec_full = lax.all_gather(vectors.astype(bf16), ("seq", "dp"), axis=0, tiled=True)
-    vec_float = vec_full.astype(f32)
-    pieces = [vec_float[index * model_width : (index + 1) * model_width] for index in range(8)]
+    results = forward_call(mesh, tokens, positions, attn_weights, ffn_in, ffn_out, vectors)
+    attn_full = results[0].reshape(4, model_width, model_width)
+    in_full = results[1].reshape(model_width, -1)
+    out_full = results[2].reshape(-1, model_width)
+    vec_float = results[3]
+    pieces = [vec_float[index] for index in range(8)]
     bias_query, bias_value, bias_out, bias_feed, gain_one, shift_one, gain_two, shift_two = pieces
-    bias_inner = vec_float[8 * model_width :]
-    token_high = tokens.astype(bf16)
-    token_rest = (tokens - token_high.astype(f32)).astype(bf16)
-    flat_low = lax.all_to_all(token_high, "seq", 0, 1, tiled=True).reshape(rows, model_width)
-    flat_rest = lax.all_to_all(token_rest, "seq", 0, 1, tiled=True).reshape(rows, model_width)
-    flat_tokens = flat_low.astype(f32) + flat_rest.astype(f32)
+    flat_low = results[4].reshape(rows, model_width)
+    query_low, key_low, value_low = (part.reshape(rows, model_width) for part in results[5:8])
+    norm_all = results[8].reshape(rows, model_width)
+    token_slot_low, context_slot, query_slot, first_low = (results[10][k] for k in range(4))
+    normal_one, first_norm, inverse_one = (results[11][k] for k in range(3))
+    active_low = results[12]
+    slope = results[13]
     first_own = lax.axis_index("seq") * own
     my_places = lax.dynamic_slice_in_dim(positions, first_own, own, 0)
     my_counts = lax.dynamic_slice_in_dim(counts, first_own, own, 0)
@@ -87,18 +730,6 @@
     hit_low = hit.astype(bf16)
     live = jnp.arange(slots, dtype=jnp.int32)[None, :] < my_counts[:, None]
 
-    def pick(dense):
-        return jnp.einsum(
-            "sjl,sld->sjd",
-            hit_low,
-            dense.reshape(own, length, -1),
-            preferred_element_type=f32,
-        ).reshape(own * slots, -1)
-
-    projected = jnp.einsum("rd,kde->kre", flat_low, attn_full[:3], preferred_element_type=f32)
-    query_low = (projected[0] + bias_query).astype(bf16)
-    key_low = projected[1].astype(bf16)
-    value_low = (projected[2] + bias_value).astype(bf16)
     query_heads = query_low.reshape(own, length, head_count, head_size)
     key_heads = key_low.reshape(own, length, head_count, head_size)
     value_heads = value_low.reshape(own, length, head_count, head_size)
@@ -106,40 +737,20 @@
     def softmax_of(query_part):
         scores = (
             jnp.einsum("sqhe,skhe->shqk", query_part, key_heads, preferred_element_type=f32)
-            * score_scale
         )
         exponent = jnp.exp(scores - jnp.max(scores, -1, keepdims=True))
         return exponent / jnp.sum(exponent, -1, keepdims=True)
 
-    probs_all = softmax_of(query_heads).astype(bf16)
-    context = jnp.einsum("shqk,skhe->sqhe", probs_all, value_heads, preferred_element_type=f32)
-    context_low = context.reshape(rows, model_width).astype(bf16)
-
-    def front(token_part, context_part):
-        attended = jnp.dot(context_part, attn_full[3], preferred_element_type=f32) + bias_out
-        return layer_norm(token_part + attended, gain_one, shift_one)
-
-    def inner_of(low):
-        return jnp.dot(low, in_full, preferred_element_type=f32) + bias_inner
-
     def feed_of(active):
-        return jnp.dot(active.astype(bf16), out_full, preferred_element_type=f32) + bias_feed
-
-    norm_all = front(flat_tokens, context_low)
-    feed_all = feed_of(gelu_exact(inner_of(norm_all.astype(bf16))))
+        return jnp.dot(active, out_full, preferred_element_type=f32) + bias_feed
+
+    feed_all = feed_of(results[9].reshape(rows, -1))
     output = layer_norm(norm_all + feed_all, gain_two, shift_two)
     output = lax.all_to_all(
         output.astype(bf16).reshape(own, length, model_width), "seq", 1, 0, tiled=True
     ).astype(f32)
 
-    context_slot = pick(context_low).astype(bf16)
-    token_slot = pick(flat_low) + pick(flat_rest)
-    attended = jnp.dot(context_slot, attn_full[3], preferred_element_type=f32) + bias_out
-    first_norm, first_pull = jax.vjp(layer_norm, token_slot + attended, gain_one, shift_one)
-    first_low = first_norm.astype(bf16)
-    active, gelu_pull = jax.vjp(gelu_exact, inner_of(first_low))
-    active_low = active.astype(bf16)
-    feed_out = feed_of(active)
+    feed_out = feed_of(active_low)
     _, second_pull = jax.vjp(layer_norm, first_norm + feed_out, gain_two, shift_two)
     slot_grad = jnp.where(live[:, :, None], my_cotangent, 0.0).reshape(own * slots, model_width)
     grad_sum_two, grad_gain_two, grad_shift_two = second_pull(slot_grad)
@@ -147,14 +758,20 @@
     grad_bias_feed = column_sum(feed_back)
     grad_out_matrix = jnp.einsum("rf,rd->fd", active_low, feed_back, preferred_element_type=f32)
     grad_active = jnp.einsum("rd,fd->rf", feed_back, out_full, preferred_element_type=f32)
-    (grad_inner,) = gelu_pull(grad_active)
-    inner_back = grad_inner.astype(bf16)
+    inner_back = (grad_active * slope).astype(bf16)
     grad_bias_inner = column_sum(inner_back)
     grad_in_matrix = jnp.einsum("rd,rf->df", first_low, inner_back, preferred_element_type=f32)
     grad_first = grad_sum_two + jnp.einsum(
         "rf,df->rd", inner_back, in_full, preferred_element_type=f32
     )
-    grad_sum_one, grad_gain_one, grad_shift_one = first_pull(grad_first)
+    scaled = grad_first * gain_one
+    grad_sum_one = inverse_one * (
+        scaled
+        - jnp.mean(scaled, -1, keepdims=True)
+        - normal_one * jnp.mean(scaled * normal_one, -1, keepdims=True)
+    )
+    grad_gain_one = column_sum(grad_first * normal_one)
+    grad_shift_one = column_sum(grad_first)
     attended_back = grad_sum_one.astype(bf16)
     grad_bias_out = column_sum(attended_back)
     grad_attn_out = jnp.einsum(
@@ -164,7 +781,7 @@
         "re,de->rd", attended_back, attn_full[3], preferred_element_type=f32
     ).astype(bf16)
     context_back = context_back.reshape(own, slots, head_count, head_size)
-    query_slot = pick(query_low).astype(bf16).reshape(own, slots, head_count, head_size)
+    query_slot = query_slot.reshape(own, slots, head_count, head_size)
     attn_probs = softmax_of(query_slot)
     probs_low = attn_probs.astype(bf16)
     grad_probs = jnp.einsum(
@@ -184,10 +801,8 @@
     value_back = value_back.astype(bf16).reshape(rows, model_width)
     key_back = (
         jnp.einsum("shqk,sqhe->skhe", scores_back, query_slot, preferred_element_type=f32)
-        * score_scale
     )
     key_back = key_back.astype(bf16).reshape(rows, model_width)
-    token_slot_low = pick(flat_low).astype(bf16)
     grad_qkv = jnp.stack(
         [
             jnp.einsum("rd,re->de", token_slot_low, query_back, preferred_element_type=f32),
@@ -306,7 +921,7 @@
 
 def solution(mesh):
     return jax.shard_map(
-        body,
+        functools.partial(body, mesh),
         mesh=mesh,
         in_specs=(
             P("dp", "seq", None),

time: 747 us -> 687 us (0.920)
  Pallas kernels: 0 us -> 139 us
  matrix products: 160 us -> 56.6 us
  blocking collectives: 213 us -> 136 us
  local copies, waits for them, and re-layouts: 78.9 us -> 49 us
  waiting for transfers between devices: 206 us -> 231 us
  other arithmetic: 47.3 us -> 36.1 us
    pallas_call x0 -> x1, Pallas kernels: none -> 139 us  [forward_call(): pl.pallas_call(functools.partial(forward_kernel, place, vec_rows, vec_cou...]
    dot_general x13 -> x2, matrix products: 95.8 us -> 14.4 us  [feed_of(): return jnp.dot(active, out_full, preferred_element_type=f32) + bias_feed]
    unnamed x2 -> x1, blocking collectives: 108 us -> 56.8 us
    reduce_scatter x2, waiting for transfers between devices: 187 us -> 220 us  [scatter(): lax.psum_scatter(part.astype(bf16), ('seq', 'dp'), scatter_dimension=axis...]
    all_to_all x1 -> x0, blocking collectives: 26 us -> none  [body(): lax.all_to_all(token_high, 'seq', 0, 1, tiled=True)]
    squeeze x3 -> x0, local copies, waits for them, and re-layouts: 12.2 us -> none  [the longest x1 6.19 us: body(): value_low = (projected[2] + bias_value).astype(bf16)]
    sub x1, matrix products: 15.7 us -> 6.14 us  [softmax_of(): exponent = jnp.exp(scores - jnp.max(scores, -1, keepdims=True))]
    unnamed x177 -> x105, local copies, waits for them, and re-layouts: 24.9 us -> 16.3 us
  transfers between devices with their start and end apart: 9 -> 5, of which waited for: 4 -> 4; matrix products, arithmetic and copies ran while one was open for 26% -> 6% of each run, Pallas kernels for 0% -> 0%
where the time goes in v2:
time: 687 us; the launch traced here: 677 us
  waiting for transfers between devices  231 us (34%)
  Pallas kernels  139 us (20%)
  blocking collectives  136 us (20%)
  matrix products  56.6 us (8%)
  local copies, waits for them, and re-layouts  49 us (7%)
  other arithmetic  36.1 us (5%)
  between operations  20.4 us (3%)
  starting transfers between devices  8.22 us (1%)
    reduce_scatter x2, waiting for transfers between devices, scatter(): lax.psum_scatter(part.astype(bf16), ('seq', 'dp'), scatter_dimension=axis...  220 us
    pallas_call x1, Pallas kernels, forward_call(): pl.pallas_call(functools.partial(forward_kernel, place, vec_rows, vec_cou...  139 us
    unnamed x1, blocking collectives  56.8 us
    psum x1, blocking collectives, body(): lax.psum(sum((jnp.sum(total * total) for total in shares)), ('seq', 'dp'))  40 us
    psum x1, blocking collectives, body(): lamb_sq = lax.psum(jnp.stack([weight_sq, dir_sq]), ('seq', 'dp'))  39.4 us
    unnamed x105, local copies, waits for them, and re-layouts  16.3 us
    dot_general x2, matrix products, feed_of(): return jnp.dot(active, out_full, preferred_element_type=f32) + bias_feed  14.4 us
  transfers between devices with their start and end apart: 5, of which 4 were waited for; matrix products, arithmetic and copies ran while one was open for 6% of the time, Pallas kernels for 0%

profile of v2, /device:TPU:0, one launch (start us, length us, event | category | flops | bytes accessed | tf_op | source)
XLA Modules:
  0.0 677.2 jit_solution(8418122021644159853)
XLA Ops:
  9.4 139.4 %shard_map.343 = (bf16[4,2,2,2,2,48,768]{6,5,4,3,2,1,0:T(8,128)(2,1)}, bf16[2,2,2,2,48,3072]{5,4,3,2,1,0:T(8,128)(2,1)}, bf16[2,2,2,2,192,768]{5,4,3,2,1,0:T(8,1...) custom-call(f32[8,128,768]{2,1,0:T(8,128)} %tokens_ref.1, ...), custom_call_target="tpu_custom_call" | custom-call | tf_op jit(solution)/shard_map/pallas_call | solution.py:613
  151.8 4.6 fusion.74
  156.7 2.0 fusion.67
  160.6 1.5 fusion.80
  162.4 2.2 fusion.21
  165.5 2.5 fusion.14
  168.0 1.7 copy.64
  169.7 2.7 copy.68
  172.5 4.1 fusion.71
  177.8 1.9 copy.67
  179.7 1.9 reshape.214
  181.6 6.1 fusion.75
  187.7 4.4 fusion.79
  192.9 1.8 multiply_reduce_fusion
  195.8 1.9 fusion.78
  198.3 1.6 copy.74
  200.4 1.6 copy.72
  205.8 1.7 fusion.13
  208.3 3.6 copy.77
  212.0 3.3 copy.82
  216.7 4.6 convolution_convert_fusion.1
  222.2 5.1 convolution_convert_fusion
  228.0 9.8 %fusion.73 = (f32[1024]{0:T(1024)S(1)}, f32[1024,768]{1,0:T(8,128)S(1)}) fusion(f32[768]{0:T(1024)S(1)} %copy-done.34, bf16[1024,3072]{1,0:T(8,128)(2,1)} %bitcast.181, bf16[3072,768]{1,0:T(8,128)(2,1)} %bitcast.160, f32[2,512,768]{2,1,0:T(8,128)} %get-tuple-element.37), kind=kOutput, calls=%fused_computation.150 | convolution fusion | flops 4834196480 | bytes 17308672 | tf_op jit(solution)/shard_map/dot_general | solution.py:745
  238.9 2.8 copy.62
  241.7 3.6 all-to-all-start
  246.1 1.6 subtract_convert_fusion
  251.0 1.5 convolution_add_fusion
  253.2 2.8 copy.75
  255.9 5.3 all-to-all-done
  261.3 4.5 all-to-all-start.1
  267.7 56.8 %all-reduce = bf16[9216]{0:T(1024)(128)(2,1)S(1)} all-reduce(bf16[9216]{0:T(1024)(128)(2,1)S(1)} %constant_dynamic-update-slice_fusion), channel_id=5, replica_groups=mesh['seq'=4,'dp'=8] {'seq','dp'}, use_global_device_ids=true, to_apply=%region_26.27.clone | all-reduce | flops 9216 | bytes 36864
  325.2 2.7 convert_bitcast_fusion.1
  327.9 2.5 convert_bitcast_fusion
  330.4 6.5 reduce-scatter.10.cloned.1.call-done
  337.9 111.5 %reduce-scatter.6.cloned.1.call-done = bf16[24,3072]{1,0:T(8,128)(2,1)} async-done(((bf16[768,3072]{1,0:T(8,128)(2,1)}), bf16[24,3072]{1,0:T(8,128)(2,1)}) %reduce-scatter.6.cloned.1.call-update) | async-done | bytes 147472 | tf_op jit(solution)/shard_map/reduce_scatter | solution.py:854
  449.4 1.6 fusion.48
  452.9 108.0 %reduce-scatter.8.cloned.1.call-done = bf16[96,768]{1,0:T(8,128)(2,1)} async-done(((bf16[3072,768]{1,0:T(8,128)(2,1)}), bf16[96,768]{1,0:T(8,128)(2,1)}) %reduce-scatter.8.cloned.1.call-update) | async-done | bytes 147472 | tf_op jit(solution)/shard_map/reduce_scatter | solution.py:854
  561.0 1.6 fusion.49
  563.9 3.9 copy.63
  567.8 40.0 %psum.14 = f32[]{:T(128)} all-reduce(f32[]{:T(128)S(6)} %add.186), channel_id=1, replica_groups=mesh['seq'=4,'dp'=8] {'seq','dp'}, use_global_device_ids=true, to_apply=%region_28.29 | all-reduce | flops 1 | bytes 8 | tf_op jit(solution)/shard_map/psum | solution.py:864
  608.5 2.4 multiply_reduce_fusion.10
  611.0 2.7 multiply_reduce_fusion.8
  613.7 1.6 multiply_reduce_fusion.9
  618.0 2.0 copy.76
  620.0 39.4 %psum.15 = f32[2,6]{1,0:T(2,128)S(1)} all-reduce(f32[2,6]{1,0:T(2,128)S(1)} %pad_maximum_fusion.1), channel_id=1, replica_groups=mesh['seq'=4,'dp'=8] {'seq','dp'}, use_global_device_ids=true, to_apply=%region_35.36 | all-reduce | flops 12 | bytes 96 | tf_op jit(solution)/shard_map/psum | solution.py:887
  663.2 2.0 fusion.60
  665.2 2.1 fusion.61
  667.3 2.1 fusion.62
  (160 shorter events, 35.5 us)
Async XLA Ops:
  7.2 329.7 %reduce-scatter.10.cloned.1.call-start = ((), (), s32[]{:S(2)}) async-start(), calls=%async_computation.7 | async-start | bytes 4866048
  149.7 6.7 copy-start.33
  150.9 9.7 %slice-start = ((s8[4718592]{0:T(1024)(128)(4,1)}), s8[524288]{0:T(1024)(128)(4,1)S(1)}, s32[]{:S(2)}) async-start(s8[4718592]{0:T(1024)(128)(4,1)} %bitcast.161), calls=%async_computation.8 | async-start | bytes 1048576
  151.8 8.9 %slice-start.1 = ((s8[4718592]{0:T(1024)(128)(4,1)}), s8[4194304]{0:T(1024)(128)(4,1)S(1)}, s32[]{:S(2)}) async-start(s8[4718592]{0:T(1024)(128)(4,1)} %bitcast.161), calls=%async_computation.9 | async-start | bytes 8388608
  151.8 10.4 %slice-start.2 = ((s8[4718592]{0:T(1024)(128)(4,1)}), s8[4194304]{0:T(1024)(128)(4,1)S(1)}, s32[]{:S(2)}) async-start(s8[4718592]{0:T(1024)(128)(4,1)} %bitcast.182), calls=%async_computation.10 | async-start | bytes 8388608
  156.6 4.0 copy-start.8
  159.5 2.7 slice-start.3
  160.6 1.6 copy-start.4
  160.6 1.8 copy-start.19
  162.2 2.5 copy-start.1
  187.7 4.7 copy-start
  187.7 5.2 copy-start.15
  187.7 5.2 copy-start.21
  187.7 5.2 copy-start.24
  195.8 1.9 copy-start.6
  200.3 2.1 copy-start.11
  200.3 2.1 copy-start.41
  202.4 1.5 copy-start.13
  205.3 2.1 copy-start.3
  205.8 2.5 copy-start.7
  215.2 1.4 copy-start.2
  215.3 234.1 %reduce-scatter.6.cloned.1.call-start = ((), (), s32[]{:S(2)}) async-start(), calls=%async_computation.5 | async-start | bytes 4866048 | tf_op jit(solution)/shard_map/reduce_scatter | solution.py:854
  221.3 339.7 %reduce-scatter.8.cloned.1.call-start = ((), (), s32[]{:S(2)}) async-start(), calls=%async_computation.6 | async-start | bytes 4866048 | tf_op jit(solution)/shard_map/reduce_scatter | solution.py:854
  241.7 19.6 %all-to-all-start = ((bf16[2,512,768]{2,0,1:T(2,128)(2,1)}), bf16[2,512,768]{2,0,1:T(2,128)(2,1)S(1)}, u32[]{:S(2)}, u32[]{:S(2)}) async-start(bf16[2,512,768]{2,0,1:T(2,128)(2,1)} %copy.62), calls=%async_computation | async-start | bytes 3145728 | tf_op jit(solution)/shard_map/all_to_all | solution.py:749
  245.2 2.5 copy-start.14
  245.3 2.4 copy-start.18
  249.2 1.4 copy-start.12
  249.2 1.8 copy-start.17
  253.1 12.7 %copy-start.35 = (bf16[12,64]{1,0:T(8,128)(2,1)S(1)}, bf16[12,64]{1,0:T(8,128)(2,1)}, u32[]{:S(2)}) copy-start(bf16[12,64]{1,0:T(8,128)(2,1)} %get-tuple-element.112) | copy-start | bytes 4612
  253.1 12.8 %copy-start.26 = (bf16[12,64]{1,0:T(8,128)(2,1)S(1)}, bf16[12,64]{1,0:T(8,128)(2,1)}, u32[]{:S(2)}) copy-start(bf16[12,64]{1,0:T(8,128)(2,1)} %get-tuple-element.110) | copy-start | bytes 4612
  253.1 13.3 %copy-start.31 = (bf16[768]{0:T(1024)(128)(2,1)S(1)}, bf16[768]{0:T(1024)(128)(2,1)}, u32[]{:S(2)}) copy-start(bf16[768]{0:T(1024)(128)(2,1)} %get-tuple-element.89) | copy-start | bytes 4612
  253.1 13.5 %copy-start.30 = (bf16[768]{0:T(1024)(128)(2,1)S(1)}, bf16[768]{0:T(1024)(128)(2,1)}, u32[]{:S(2)}) copy-start(bf16[768]{0:T(1024)(128)(2,1)} %get-tuple-element.87) | copy-start | bytes 4612
  253.1 13.7 %copy-start.37 = (bf16[768]{0:T(1024)(128)(2,1)S(1)}, bf16[768]{0:T(1024)(128)(2,1)}, u32[]{:S(2)}) copy-start(bf16[768]{0:T(1024)(128)(2,1)} %get-tuple-element.50) | copy-start | bytes 4612
  253.1 13.9 %copy-start.36 = (bf16[768]{0:T(1024)(128)(2,1)S(1)}, bf16[768]{0:T(1024)(128)(2,1)}, u32[]{:S(2)}) copy-start(bf16[768]{0:T(1024)(128)(2,1)} %get-tuple-element.55) | copy-start | bytes 4612
  253.1 14.1 %copy-start.29 = (bf16[768]{0:T(1024)(128)(2,1)S(1)}, bf16[768]{0:T(1024)(128)(2,1)}, u32[]{:S(2)}) copy-start(bf16[768]{0:T(1024)(128)(2,1)} %get-tuple-element.52) | copy-start | bytes 4612
  253.2 14.3 %copy-start.28 = (bf16[768]{0:T(1024)(128)(2,1)S(1)}, bf16[768]{0:T(1024)(128)(2,1)}, u32[]{:S(2)}) copy-start(bf16[768]{0:T(1024)(128)(2,1)} %get-tuple-element.85) | copy-start | bytes 4612
  261.3 66.6 %all-to-all-start.1 = ((bf16[2,512,768]{2,0,1:T(2,128)(2,1)}), bf16[2,512,768]{2,0,1:T(2,128)(2,1)}, u32[]{:S(2)}, u32[]{:S(2)}) async-start(bf16[2,512,768]{2,0,1:T(2,128)(2,1)} %copy.75), calls=%async_computation.1 | async-start | bytes 3145728 | tf_op jit(solution)/shard_map/all_to_all | solution.py:835
  324.5 3.4 copy-start.25
  337.9 225.3 %copy-start.16 = (bf16[24,4,768]{2,1,0:T(4,128)(2,1)}, bf16[24,4,768]{2,1,0:T(4,128)(2,1)S(1)}, u32[]{:S(2)}) copy-start(bf16[24,4,768]{2,1,0:T(4,128)(2,1)S(1)} %reshape.226) | copy-start | bytes 442372
  563.9 47.1 %copy-start.9 = (f32[96,768]{1,0:T(8,128)S(1)}, f32[96,768]{1,0:T(8,128)}, u32[]{:S(2)}) copy-start(f32[96,768]{1,0:T(8,128)} %out_ref.1) | copy-start | bytes 884740
  608.5 5.1 copy-start.10
  608.5 5.1 copy-start.20
  608.5 5.1 copy-start.22
  608.5 5.1 copy-start.23
  618.0 43.8 %copy-start.32 = (f32[288]{0:T(512)S(1)}, f32[288]{0:T(512)}, u32[]{:S(2)}) copy-start(f32[288]{0:T(512)} %param.23) | copy-start | bytes 3460
  618.0 43.8 %copy-start.38 = (f32[288]{0:T(512)S(1)}, f32[288]{0:T(512)}, u32[]{:S(2)}) copy-start(f32[288]{0:T(512)} %param.31) | copy-start | bytes 3460
  618.0 43.8 %copy-start.39 = (f32[288]{0:T(512)S(1)}, f32[288]{0:T(512)}, u32[]{:S(2)}) copy-start(f32[288]{0:T(512)} %param.27) | copy-start | bytes 3460
  659.4 10.0 %copy-start.40 = (f32[2,6]{1,0:T(2,128)}, f32[2,6]{1,0:T(2,128)S(1)}, u32[]{:S(2)}) copy-start(f32[2,6]{1,0:T(2,128)S(1)} %sqrt.22) | copy-start | bytes 148
  (3 other events, 2.3 us)
Sparse Core Ops, SparseCore 0:
  215.4 121.4 reduce-scatter.9
  343.3 106.0 reduce-scatter.5
  454.9 106.0 reduce-scatter.7
